TPU v7x, 32 devices: a whole 2x2x4 slice. The times are simulated.
32 devices in a mesh: ax: 8 (over y, x, core), rad: 4 (over z).
Axes of the slice: x: 2, y: 2, z: 4, core: 2. Of those that a mesh axis runs over, the one named last changes fastest.
Arguments:
- leaf_maps: float32 [16, 8, 512, 512], P('ax', 'rad'), may hold values from -0.5 to 22, as said below
- leaf_fluxes: float32 [16, 8, 512], P('ax', 'rad'), may hold values from -6 to 6
Outputs:
- merged_maps: float32 [8, 4, 512, 2048], P('ax', 'rad')
- merged_fluxes: float32 [8, 4, 512], P('ax', 'rad')
Inputs may be any that keep to these rules, and one draw needn't show every extreme that they name: `leaf_maps`: every leaf map is symmetric and positive definite, with smallest eigenvalue at least 0.5.
All inputs are finite; a program needn't handle non-finite values.
Results may differ from a plain program's by a relative error of at most 0.0003.
Values sent between devices are 32-bit elements; how exact they have to be, the bound alone decides.
A program may use at most 192 MiB of HBM per device.

v0:
```python
import jax
import jax.numpy as jnp
from jax import lax
from jax.sharding import PartitionSpec as P


def swapped(value, axis, bit):
    mask = 2**bit
    pairs = [(source, source ^ mask) for source in range(lax.axis_size(axis))]
    return lax.ppermute(value, axis, pairs)


def leaf_points(axial_leaf, radial_leaf, extent):
    points = []
    for offset in range(extent):
        points.append((0, axial_leaf * extent, radial_leaf * extent + offset))
    for offset in range(extent):
        points.append((0, (axial_leaf + 1) * extent, radial_leaf * extent + offset))
    for offset in range(extent):
        points.append((1, radial_leaf * extent, axial_leaf * extent + offset))
    for offset in range(extent):
        points.append((1, (radial_leaf + 1) * extent, axial_leaf * extent + offset))
    return points


def shifted(points, axial_shift, radial_shift):
    result = []
    for facing, line_pos, coordinate in points:
        if facing == 0:
            result.append((0, line_pos + axial_shift, coordinate + radial_shift))
        else:
            result.append((1, line_pos + radial_shift, coordinate + axial_shift))
    return result


def merge_plan(lower_pts, upper_pts):
    upper_place = {}
    for number, location in enumerate(upper_pts):
        upper_place[location] = number
    lower_inner = [number for number, location in enumerate(lower_pts) if location in upper_place]
    upper_inner = [upper_place[lower_pts[number]] for number in lower_inner]
    lower_outer = [
        number for number, location in enumerate(lower_pts) if location not in upper_place
    ]
    inner_set = set(upper_inner)
    upper_outer = [number for number in range(len(upper_pts)) if number not in inner_set]
    merged = [lower_pts[number] for number in lower_outer] + [
        upper_pts[number] for number in upper_outer
    ]
    return ((lower_inner, upper_inner, lower_outer, upper_outer), merged)


def layouts(extent):
    plan_low, pair_low = merge_plan(leaf_points(0, 0, extent), leaf_points(1, 0, extent))
    plan_high, pair_high = merge_plan(leaf_points(0, 1, extent), leaf_points(1, 1, extent))
    plan_block, block_pts = merge_plan(pair_low, pair_high)
    plan_first, first_pts = merge_plan(block_pts, shifted(block_pts, 0, 2 * extent))
    plan_second, second_pts = merge_plan(first_pts, shifted(first_pts, 2 * extent, 0))
    return (plan_low, plan_high, plan_block, plan_first, plan_second)


def find_runs(indices):
    spans = []
    opening = indices[0]
    extent = 1
    for former, latter in zip(indices[:-1], indices[1:]):
        if latter == former + 1:
            extent += 1
        else:
            spans.append((opening, extent))
            opening = latter
            extent = 1
    spans.append((opening, extent))
    return spans


def select_runs(values, indices, dimension):
    pieces = [
        lax.slice_in_dim(values, opening, opening + extent, axis=dimension)
        for opening, extent in find_runs(indices)
    ]
    if len(pieces) == 1:
        return pieces[0]
    return jnp.concatenate(pieces, axis=dimension)


def block_of(matrix, row_list, column_list):
    return select_runs(select_runs(matrix, row_list, 0), column_list, 1)


def eliminate(schur_block, coupling, hint):
    factor = jnp.linalg.cholesky(schur_block)
    scaled_rows = lax.linalg.triangular_solve(
        factor, coupling, left_side=False, lower=True, transpose_a=True
    )
    solved = lax.linalg.triangular_solve(factor, hint[:, None], left_side=True, lower=True)[:, 0]
    return (scaled_rows, solved)


def place_minus(flag, square, product):
    negated = -product
    width = square.shape[1]
    start = flag * width
    window = lax.dynamic_slice_in_dim(negated, start, width, 1)
    return lax.dynamic_update_slice_in_dim(negated, window + square, start, 1)


def dense_merge(lower_map, lower_flux, upper_map, upper_flux, plan):
    lower_inner, upper_inner, lower_outer, upper_outer = plan
    schur_block = block_of(lower_map, lower_inner, lower_inner) + block_of(
        upper_map, upper_inner, upper_inner
    )
    coupling = jnp.concatenate(
        [
            block_of(lower_map, lower_outer, lower_inner),
            block_of(upper_map, upper_outer, upper_inner),
        ],
        axis=0,
    )
    hint = select_runs(lower_flux, lower_inner, 0) + select_runs(upper_flux, upper_inner, 0)
    scaled_rows, solved = eliminate(schur_block, coupling, hint)
    lower_count = len(lower_outer)
    negated = -jnp.dot(scaled_rows, scaled_rows.T, precision=lax.Precision.HIGHEST)
    negated = negated.at[:lower_count, :lower_count].add(
        block_of(lower_map, lower_outer, lower_outer)
    )
    merged_map = negated.at[lower_count:, lower_count:].add(
        block_of(upper_map, upper_outer, upper_outer)
    )
    outer_flux = jnp.concatenate(
        [select_runs(lower_flux, lower_outer, 0), select_runs(upper_flux, upper_outer, 0)], axis=0
    )
    merged_flux = outer_flux - jnp.dot(scaled_rows, solved, precision=lax.Precision.HIGHEST)
    return (merged_map, merged_flux)


def eliminate_columns(lower_cols, upper_cols, hint, plan):
    lower_inner, upper_inner, lower_outer, upper_outer = plan
    schur_block = select_runs(lower_cols, lower_inner, 0) + select_runs(upper_cols, upper_inner, 0)
    coupling = jnp.concatenate(
        [select_runs(lower_cols, lower_outer, 0), select_runs(upper_cols, upper_outer, 0)], axis=0
    )
    return eliminate(schur_block, coupling, hint)


def full_first(own_map, own_flux, other_map, other_flux, radial_bit, plan):
    return lax.cond(
        radial_bit == 0,
        lambda: dense_merge(own_map, own_flux, other_map, other_flux, plan),
        lambda: dense_merge(other_map, other_flux, own_map, own_flux, plan),
    )


def interface_parts(pair_map, pair_flux, flag, plan):
    lower_inner, upper_inner, lower_outer, upper_outer = plan
    return lax.cond(
        flag == 0,
        lambda: (select_runs(pair_map, lower_inner, 1), select_runs(pair_flux, lower_inner, 0)),
        lambda: (select_runs(pair_map, upper_inner, 1), select_runs(pair_flux, upper_inner, 0)),
    )


def outer_parts(pair_map, pair_flux, axial_bit, radial_bit, plan, extent):
    lower_inner, upper_inner, lower_outer, upper_outer = plan

    def pick_side(outer_list):
        rows = lax.dynamic_slice_in_dim(
            select_runs(pair_map, outer_list, 0), radial_bit * 4 * extent, 4 * extent, 0
        )
        flux_rows = lax.dynamic_slice_in_dim(
            select_runs(pair_flux, outer_list, 0), radial_bit * 4 * extent, 4 * extent, 0
        )
        return (select_runs(rows, outer_list, 1), flux_rows)

    return lax.cond(axial_bit == 0, lambda: pick_side(lower_outer), lambda: pick_side(upper_outer))


def finish_second(
    own_cols,
    own_hint,
    far_cols,
    far_hint,
    own_block,
    own_outer,
    axial_bit,
    radial_bit,
    plan,
    extent,
):
    hint_sum = own_hint + far_hint
    scaled_rows, solved = lax.cond(
        axial_bit == 0,
        lambda: eliminate_columns(own_cols, far_cols, hint_sum, plan),
        lambda: eliminate_columns(far_cols, own_cols, hint_sum, plan),
    )
    quarter = 2 * axial_bit + radial_bit
    own_scaled = lax.dynamic_slice_in_dim(scaled_rows, quarter * 4 * extent, 4 * extent, 0)
    merged_map = place_minus(
        axial_bit, own_block, jnp.dot(own_scaled, scaled_rows.T, precision=lax.Precision.HIGHEST)
    )
    merged_flux = own_outer - jnp.dot(own_scaled, solved, precision=lax.Precision.HIGHEST)
    return (merged_map[None, None], merged_flux[None, None])


def shards(leaf_maps, leaf_fluxes):
    extent = leaf_maps.shape[2] // 4
    plan_low, plan_high, plan_block, plan_first, plan_second = layouts(extent)
    axial_count = lax.axis_size("ax")
    radial_count = lax.axis_size("rad")
    axial_top = axial_count.bit_length() - 1 - 1
    radial_top = radial_count.bit_length() - 1 - 1
    axial_bit = (lax.axis_index("ax") // (axial_count // 2)).astype(jnp.int32)
    radial_bit = (lax.axis_index("rad") // (radial_count // 2)).astype(jnp.int32)
    lower_pair = dense_merge(
        leaf_maps[0, 0], leaf_fluxes[0, 0], leaf_maps[1, 0], leaf_fluxes[1, 0], plan_low
    )
    upper_pair = dense_merge(
        leaf_maps[0, 1], leaf_fluxes[0, 1], leaf_maps[1, 1], leaf_fluxes[1, 1], plan_high
    )
    block_map, block_flux = dense_merge(
        lower_pair[0], lower_pair[1], upper_pair[0], upper_pair[1], plan_block
    )
    other_map, other_flux = swapped((block_map, block_flux), "rad", radial_top)
    first_map, first_flux = full_first(
        block_map, block_flux, other_map, other_flux, radial_bit, plan_first
    )
    far_map, far_flux = swapped((first_map, first_flux), "ax", axial_top)
    own_cols, own_hint = interface_parts(first_map, first_flux, axial_bit, plan_second)
    far_cols, far_hint = interface_parts(far_map, far_flux, 1 - axial_bit, plan_second)
    own_block, own_outer = outer_parts(
        first_map, first_flux, axial_bit, radial_bit, plan_second, extent
    )
    return finish_second(
        own_cols,
        own_hint,
        far_cols,
        far_hint,
        own_block,
        own_outer,
        axial_bit,
        radial_bit,
        plan_second,
        extent,
    )


def solution(mesh):
    in_specs = (P("ax", "rad", None, None), P("ax", "rad", None))
    out_specs = (P("ax", "rad", None, None), P("ax", "rad", None))
    return jax.shard_map(shards, mesh=mesh, in_specs=in_specs, out_specs=out_specs, check_vma=False)
```

profile of v0, /device:TPU:0, one launch (start us, length us, event | category | flops | bytes accessed | tf_op | source)
XLA Modules:
  0.0 891.5 jit_solution(5440953302711624963)
XLA Ops:
  6.9 11.7 %cholesky.649 = f32[128,128]{1,0:T(8,128)S(1)} custom-call(f32[128,128]{1,0:T(8,128)S(1)} %fusion.215), custom_call_target="Cholesky" | custom-call | tf_op jit(solution)/shard_map/jit(cholesky)/cholesky | solution.py:92
  34.1 11.7 %cholesky.638 = f32[128,128]{1,0:T(8,128)S(1)} custom-call(f32[128,128]{1,0:T(8,128)S(1)} %fusion.218), custom_call_target="Cholesky" | custom-call | tf_op jit(solution)/shard_map/jit(cholesky)/cholesky | solution.py:92
  47.1 10.6 %custom-call.81 = f32[1,128,128]{1,2,0:T(8,128)} custom-call(f32[1,128,128]{2,1,0:T(8,128)S(1)} %fusion.209), custom_call_target="InvertDiagBlocksLowerTriangular" | custom-call | tf_op jit(solution)/shard_map/triangular_solve/custom-call.14 | solution.py:93
  72.0 11.7 %cholesky.662 = f32[128,128]{1,0:T(8,128)S(1)} custom-call(f32[128,128]{1,0:T(8,128)S(1)} %cholesky.717), custom_call_target="Cholesky" | custom-call | tf_op jit(solution)/shard_map/jit(cholesky)/cholesky | solution.py:92
  83.8 10.8 %custom-call.83 = f32[1,128,128]{1,2,0:T(8,128)} custom-call(f32[1,128,128]{2,1,0:T(8,128)S(1)} %get-tuple-element.542), custom_call_target="InvertDiagBlocksLowerTriangular" | custom-call | tf_op jit(solution)/shard_map/jit(cholesky)/cholesky/custom-call.0 | solution.py:92
  96.8 11.7 %cholesky.672 = f32[128,128]{1,0:T(8,128)S(1)} custom-call(f32[128,128]{1,0:T(8,128)S(1)} %convolution_subtract_fusion.15), custom_call_target="Cholesky" | custom-call | tf_op jit(solution)/shard_map/jit(cholesky)/cholesky | solution.py:92
  117.7 21.1 %custom-call.46 = f32[2,128,128]{1,2,0:T(8,128)} custom-call(f32[2,128,128]{2,1,0:T(8,128)} %get-tuple-element.275), custom_call_target="InvertDiagBlocksLowerTriangular" | custom-call | tf_op jit(solution)/shard_map/triangular_solve | solution.py:93
  159.2 178.4 %collective-permute-done.1 = f32[1024]{0:T(1024)S(1)} collective-permute-done((f32[1024]{0:T(1024)S(1)}, f32[1024]{0:T(1024)S(1)}, u32[]{:S(2)}, u32[]{:S(2)}) %collective-permute-start.1) | collective-permute-done | bytes 4128 | tf_op jit(solution)/shard_map/ppermute | solution.py:10
  337.6 120.9 %conditional.5 = (f32[1536,1536]{0,1:T(8,128)}, f32[1536]{0:T(1024)}, f32[1536,1536]{1,0:T(8,128)}, (f32[1536,1536]{1,0:T(8,128)}, f32[1536]{0:T(1024)S(1)})) conditional(s32[]{:T(128)} %convert_element_type.13, (f32[1024,1024]{0,1:T(8,128)}, f32[1024,1024]{0,1:T(8,128)}, f32[1024]{0:T(1024)S(1)}, f32[1024]{0:T(1024)S(1)}) %tuple.96, ...), branch_computations={%region_6.14_spmd, %region_7.15_spmd} | conditional | flops 8246512128 | bytes 163840784 | solution.py:147
  347.3 11.7 %cholesky.477 = f32[128,128]{1,0:T(8,128)S(1)} custom-call(f32[128,128]{1,0:T(8,128)S(1)} %cholesky.714), custom_call_target="Cholesky" | custom-call | tf_op jit(solution)/shard_map/cond/branch_1_fun/jit(cholesky)/cholesky | solution.py:92
  359.0 9.8 %custom-call.66 = f32[1,128,128]{1,2,0:T(8,128)S(1)} custom-call(f32[1,128,128]{2,1,0:T(8,128)S(1)} %get-tuple-element.510), custom_call_target="InvertDiagBlocksLowerTriangular" | custom-call | tf_op jit(solution)/shard_map/cond/branch_1_fun/jit(cholesky)/cholesky/custom-call.0 | solution.py:92
  369.4 11.7 %cholesky.487 = f32[128,128]{1,0:T(8,128)S(1)} custom-call(f32[128,128]{1,0:T(8,128)S(1)} %convolution_subtract_fusion.13), custom_call_target="Cholesky" | custom-call | tf_op jit(solution)/shard_map/cond/branch_1_fun/jit(cholesky)/cholesky | solution.py:92
  388.3 19.7 %custom-call.67 = f32[2,128,128]{1,2,0:T(8,128)S(1)} custom-call(f32[2,128,128]{2,1,0:T(8,128)S(1)} %get-tuple-element.308), custom_call_target="InvertDiagBlocksLowerTriangular" | custom-call | tf_op jit(solution)/shard_map/cond/branch_1_fun/triangular_solve/custom-call.8 | solution.py:93
  458.4 13.8 %collective-permute-start.2 = (f32[1536,1536]{1,0:T(8,128)}, f32[1536,1536]{1,0:T(8,128)}, u32[]{:S(2)}, u32[]{:S(2)}) collective-permute-start(f32[1536,1536]{1,0:T(8,128)} %get-tuple-element.335), channel_id=1, source_target_pairs={{0,16},{4,20},{8,24},{12,28},{16,0},{20,4},{24,8},{28,12},{1,17},{... | collective-permute-start | bytes 28311560 | tf_op jit(solution)/shard_map/ppermute | solution.py:10
  474.7 34.4 %conditional.9 = (f32[512,1024]{1,0:T(8,128)}, f32[512]{0:T(512)S(1)}) conditional(s32[]{:T(128)} %convert_element_type.11, (f32[1536,1536]{0,1:T(8,128)}, s32[]{:T(128)}, f32[1536]{0:T(1024)}) %tuple.101, (f32[1536,1536]{0,1:T(8,128)}, s32[]{:T(128)}, f32[1536]{0:T(1024)}) %tuple.101), branch_computations={%region_22.33_spmd, %region_23.34_spmd} | conditional | flops 3935236 | bytes 49303620 | solution.py:175
  509.1 165.7 %collective-permute-done.3 = f32[1536]{0:T(1024)S(1)} collective-permute-done((f32[1536]{0:T(1024)}, f32[1536]{0:T(1024)S(1)}, u32[]{:S(2)}, u32[]{:S(2)}) %collective-permute-start.3) | collective-permute-done | bytes 6176 | tf_op jit(solution)/shard_map/ppermute | solution.py:10
  678.7 199.6 %conditional.8 = (f32[2048,512]{0,1:T(8,128)S(1)}, f32[512]{0:T(512)S(1)}) conditional(s32[]{:T(128)} %convert_element_type.11, (f32[1536,512]{1,0:T(8,128)}, f32[1536,512]{1,0:T(8,128)S(1)}, f32[512]{0:T(512)S(1)}) %tuple.99, (f32[1536,512]{1,0:T(8,128)S(1)}, f32[1536,512]{1,0:T(8,128)}, f32[512]{0:T(512)S(1)}) %tuple.100), branch_computations={%region_12.31_spmd, %region_21.32_spmd} | conditional | flops 4440985088 | bytes 112349080 | solution.py:191
  710.5 11.7 %cholesky.572 = f32[128,128]{1,0:T(8,128)S(1)} custom-call(f32[128,128]{1,0:T(8,128)S(1)} %cholesky.698), custom_call_target="Cholesky" | custom-call | tf_op jit(solution)/shard_map/cond/branch_1_fun/jit(cholesky)/cholesky | solution.py:92
  736.5 11.7 %cholesky.591 = f32[128,128]{1,0:T(8,128)S(1)} custom-call(f32[128,128]{1,0:T(8,128)S(1)} %cholesky.702), custom_call_target="Cholesky" | custom-call | tf_op jit(solution)/shard_map/cond/branch_1_fun/jit(cholesky)/cholesky | solution.py:92
  750.7 10.0 %custom-call.77 = f32[1,128,128]{1,2,0:T(8,128)S(1)} custom-call(f32[1,128,128]{2,1,0:T(8,128)S(1)} %get-tuple-element.473), custom_call_target="InvertDiagBlocksLowerTriangular" | custom-call | tf_op jit(solution)/shard_map/cond/branch_1_fun/jit(cholesky)/cholesky | solution.py:92
  763.0 11.7 %cholesky.612 = f32[128,128]{1,0:T(8,128)S(1)} custom-call(f32[128,128]{1,0:T(8,128)S(1)} %cholesky.707), custom_call_target="Cholesky" | custom-call | tf_op jit(solution)/shard_map/cond/branch_1_fun/jit(cholesky)/cholesky | solution.py:92
  788.7 11.8 %cholesky.625 = f32[128,128]{1,0:T(8,128)S(1)} custom-call(f32[128,128]{1,0:T(8,128)S(1)} %convolution_subtract_fusion.9), custom_call_target="Cholesky" | custom-call | tf_op jit(solution)/shard_map/cond/branch_1_fun/jit(cholesky)/cholesky | solution.py:92
  804.9 14.1 %while.32 = (s32[]{:T(128)}, f32[512,512]{1,0:T(8,128)}, s32[4,2]{0,1:T(2,128)S(1)}, f32[4,128,128]{2,1,0:T(8,128)}, s32[]{:T(128)}) while((s32[]{:T(128)}, f32[512,512]{1,0:T(8,128)}, s32[4,2]{0,1:T(2,128)S(1)}, f32[4,128,128]{2,1,0:T(8,128)}, s32[]{:T(128)}) %tuple.318), condition=%wide.while_cond.12.clone, body=%wide.while_body.12.clone.sunk | while | flops 2 | bytes 132705 | solution.py:93
  819.0 40.1 %custom-call.79 = f32[4,128,128]{1,2,0:T(8,128)S(1)} custom-call(f32[4,128,128]{2,1,0:T(8,128)} %get-tuple-element.312), custom_call_target="InvertDiagBlocksLowerTriangular" | custom-call | tf_op jit(solution)/shard_map/cond/branch_1_fun/triangular_solve/custom-call.12 | solution.py:93
  (299 shorter events, 284.8 us)
Async XLA Ops:
  29.7 30.3 %copy-start.26 = (f32[1,128,128]{1,2,0:T(8,128)}, f32[1,128,128]{1,2,0:T(8,128)S(1)}, u32[]{:S(2)}) copy-start(f32[1,128,128]{1,2,0:T(8,128)S(1)} %custom-call.82) | copy-start | bytes 196612
  30.8 26.9 %copy-start.21 = (f32[1,1,128,512]{3,2,1,0:T(8,128)S(1)}, f32[1,1,128,512]{3,2,1,0:T(8,128)}, u32[]{:S(2)}) copy-start(f32[1,1,128,512]{3,2,1,0:T(8,128)} %get-tuple-element.525) | copy-start | bytes 786436
  60.1 3.7 copy-start.13
  69.4 69.4 %copy-start.9 = (f32[128,768]{0,1:T(8,128)}, f32[128,768]{0,1:T(8,128)S(1)}, u32[]{:S(2)}) copy-start(f32[128,768]{0,1:T(8,128)S(1)} %get-tuple-element.554) | copy-start | bytes 1179652
  108.5 2.7 copy-start.22
  147.7 2.4 copy-start.10
  147.7 2.4 copy-start.11
  150.1 6.5 copy-start.30
  150.1 6.5 copy-start.27
  150.1 7.1 copy-start.29
  150.1 7.2 copy-start.3
  150.2 7.7 copy-start.25
  150.2 8.3 copy-start.7
  152.6 184.9 %collective-permute-start = (f32[1024,1024]{0,1:T(8,128)}, f32[1024,1024]{0,1:T(8,128)}, u32[]{:S(2)}, u32[]{:S(2)}) collective-permute-start(f32[1024,1024]{0,1:T(8,128)} %fusion.174), channel_id=1, source_target_pairs={{0,2},{1,3},{2,0},{3,1},{4,6},{5,7},{6,4},{7,5},{8,10},{9,11},{10,... | collective-permute-start | bytes 12582920 | tf_op jit(solution)/shard_map/ppermute | solution.py:10
  159.1 178.5 %collective-permute-start.1 = (f32[1024]{0:T(1024)S(1)}, f32[1024]{0:T(1024)S(1)}, u32[]{:S(2)}, u32[]{:S(2)}) collective-permute-start(f32[1024]{0:T(1024)S(1)} %sub.33), channel_id=1, source_target_pairs={{0,2},{1,3},{2,0},{3,1},{4,6},{5,7},{6,4},{7,5},{8,10},{9,11},{10,... | collective-permute-start | bytes 12296 | tf_op jit(solution)/shard_map/ppermute | solution.py:10
  442.1 6.5 copy-start.1
  458.4 216.3 %collective-permute-start.2 = (f32[1536,1536]{1,0:T(8,128)}, f32[1536,1536]{1,0:T(8,128)}, u32[]{:S(2)}, u32[]{:S(2)}) collective-permute-start(f32[1536,1536]{1,0:T(8,128)} %get-tuple-element.335), channel_id=1, source_target_pairs={{0,16},{4,20},{8,24},{12,28},{16,0},{20,4},{24,8},{28,12},{1,17},{... | collective-permute-start | bytes 28311560 | tf_op jit(solution)/shard_map/ppermute | solution.py:10
  472.2 202.5 %collective-permute-start.3 = (f32[1536]{0:T(1024)}, f32[1536]{0:T(1024)S(1)}, u32[]{:S(2)}, u32[]{:S(2)}) collective-permute-start(f32[1536]{0:T(1024)} %get-tuple-element.227), channel_id=1, source_target_pairs={{0,16},{4,20},{8,24},{12,28},{16,0},{20,4},{24,8},{28,12},{1,17},{... | collective-permute-start | bytes 18440 | tf_op jit(solution)/shard_map/ppermute | solution.py:10
  697.2 2.0 copy-start.4
  701.6 2.5 copy-start.18
  701.6 2.5 copy-start.19
  701.6 2.5 copy-start.20
  866.4 3.6 copy-start.5
  889.1 2.0 copy-start.8
  (7 other events, 6.3 us)
where the time goes:
time: 903 us; the launch traced here: 892 us
  waiting for transfers between devices  344 us (38%)
  other arithmetic  301 us (33%)
  local copies, waits for them, and re-layouts  139 us (15%)
  matrix products  63.8 us (7%)
  loops' own time  22.7 us (3%)
  starting transfers between devices  18 us (2%)
    ppermute x4, waiting for transfers between devices, swapped(): return lax.ppermute(value, axis, pairs)  344 us
    another operation x34, other arithmetic, eliminate(): factor = jnp.linalg.cholesky(schur_block)  176 us
    another operation x16, other arithmetic, eliminate(): lax.linalg.triangular_solve(factor, coupling, left_side=False, lower=True...  106 us
    another operation x12, local copies, waits for them, and re-layouts  40 us
    cond x36, local copies, waits for them, and re-layouts  36.4 us
    slice x22, local copies, waits for them, and re-layouts, select_runs(): lax.slice_in_dim(values, opening, opening + extent, axis=dimension)  22.5 us
    another operation x15, matrix products, eliminate(): lax.linalg.triangular_solve(factor, coupling, left_side=False, lower=True...  20.4 us
    another operation x21, local copies, waits for them, and re-layouts, eliminate(): lax.linalg.triangular_solve(factor, coupling, left_side=False, lower=True...  18.3 us
  transfers between devices with their start and end apart: 4, of which 2 were waited for; matrix products, arithmetic and copies ran while one was open for 4% of the time, Pallas kernels for 0%

commit v1 on v0

v1 whole, which is shorter than its diff:
```python
import jax
import jax.numpy as jnp
from jax import lax
from jax.experimental import pallas as pl
from jax.experimental.pallas import tpu as pltpu
from jax.sharding import PartitionSpec as P

F32 = jnp.float32
VMEM_LIMIT = 56 * 1024 * 1024
NT = (((1,), (1,)), ((), ()))
NN = (((1,), (0,)), ((), ()))
TN = (((0,), (0,)), ((), ()))

ORDERS = ((0, 2, 3, 1), (0, 1, 2, 3), (2, 0, 3, 1), (0, 2, 1, 3))


def swapped(value, axis):
    count = lax.axis_size(axis)
    pairs = [(source, source ^ (count // 2)) for source in range(count)]
    return lax.ppermute(value, axis, pairs)


def halves():
    axial_bit = lax.axis_index("ax") // (lax.axis_size("ax") // 2)
    radial_bit = lax.axis_index("rad") // (lax.axis_size("rad") // 2)
    return axial_bit, radial_bit


def full_dot(a, b, dims):
    return lax.dot_general(
        a, b, dims, precision=lax.Precision.HIGHEST, preferred_element_type=F32
    )


def split(a):
    high = a.astype(jnp.bfloat16)
    low = (a - high.astype(F32)).astype(jnp.bfloat16)
    return high, low


def dot3(a, b, dims):
    a_high, a_low = split(a)
    b_high, b_low = split(b)
    total = lax.dot_general(a_high, b_low, dims, preferred_element_type=F32)
    total += lax.dot_general(a_low, b_high, dims, preferred_element_type=F32)
    return total + lax.dot_general(a_high, b_high, dims, preferred_element_type=F32)


def invert_factors(tiles):
    size = tiles[0].shape[0]
    count = size // 8
    lane = lax.broadcasted_iota(jnp.int32, (1, size), 1)
    sub = lax.broadcasted_iota(jnp.int32, (8, 1), 0)
    works = [[t[8 * i : 8 * i + 8, :] for i in range(count)] for t in tiles]
    for k in range(size):
        t0, s0 = k // 8, k % 8
        here = lane == k
        for work in works:
            row = work[t0][s0 : s0 + 1, :]
            inverse = 1.0 / work[t0][s0 : s0 + 1, k : k + 1]
            scaled = jnp.where(here, 1.0, row) * inverse
            for t in range(t0, count):
                if t == t0 and s0 == 7:
                    continue
                part = work[t]
                column = part[:, k : k + 1]
                fresh = jnp.where(here, 0.0, part) - column * scaled
                if t == t0:
                    fresh = jnp.where(sub > s0, fresh, part)
                work[t] = fresh
    results = []
    lanes = lax.broadcasted_iota(jnp.int32, (size, size), 1)
    rows = lax.broadcasted_iota(jnp.int32, (size, size), 0)
    for work in works:
        whole = jnp.concatenate(work, axis=0)
        pivots = jnp.sum(jnp.where(lanes == rows, whole, 0.0), axis=1, keepdims=True)
        unit = jnp.where(lanes < rows, whole, jnp.where(lanes == rows, 1.0, 0.0))
        results.append(unit * lax.rsqrt(pivots))
    return results


def factor_into(work, out, step):
    n = out.shape[0]
    work[:, n:] = (
        lax.broadcasted_iota(jnp.int32, (n, n), 0) == lax.broadcasted_iota(jnp.int32, (n, n), 1)
    ).astype(F32)

    @pl.loop(0, n // step)
    def _(b):
        start = pl.multiple_of(b * step, step)
        inverse = invert_factors([work[pl.ds(start, step), pl.ds(start, step)]])[0]
        panel = full_dot(inverse, work[pl.ds(start, step), :], NN)
        out[pl.ds(start, step), :] = panel[:, n:]
        lanes = lax.broadcasted_iota(jnp.int32, (step, n), 1)
        tail = jnp.where(lanes >= start + step, panel[:, :n], 0.0)
        work[...] -= full_dot(tail, panel, TN)


def call(kernel, shapes, scratch, flops, *args):
    moved = sum(a.size * 4 for a in args)
    return pl.pallas_call(
        kernel,
        out_shape=[jax.ShapeDtypeStruct(s, F32) for s in shapes],
        in_specs=[pl.BlockSpec(memory_space=pltpu.VMEM)] * len(args),
        out_specs=[pl.BlockSpec(memory_space=pltpu.VMEM)] * len(shapes),
        scratch_shapes=[pltpu.VMEM(s, F32) for s in scratch],
        compiler_params=pltpu.CompilerParams(vmem_limit_bytes=VMEM_LIMIT),
        cost_estimate=pl.CostEstimate(
            flops=flops, bytes_accessed=2 * moved, transcendentals=0
        ),
    )(*args)


def local_kernel(maps, fluxes, radial, rest, axial, outer, coupled, pairs, work, inverse, both):
    e = maps.shape[2] // 4
    axial_bit, radial_bit = halves()

    def seg(s):
        return slice(s * e, (s + 1) * e)

    schurs = [maps[0, j, seg(1), seg(1)] + maps[1, j, seg(0), seg(0)] for j in range(2)]
    factors = invert_factors(schurs)
    flux = [None, None]
    places = []
    for j in range(2):
        meeting = 3 if j == 0 else 2
        sides = [(0, meeting), (1, meeting), (0, 0), (1, 1), (0, 5 - meeting), (1, 5 - meeting)]
        places.append(sides)
        for p, (i, s) in enumerate(sides):
            coupled[seg(p), :] = maps[i, j, seg(s), seg(1 - i)]
        scaled = dot3(coupled[...], factors[j], NT)
        product = dot3(scaled, scaled, NT)
        pairs[j] = -product
        for p, (i, s) in enumerate(sides):
            for q, (k, t) in enumerate(sides):
                if i == k:
                    pairs[j, seg(p), seg(q)] += maps[i, j, seg(s), seg(t)]
        hint = fluxes[0, j, :, seg(1)] + fluxes[1, j, :, seg(0)]
        solved = full_dot(hint, factors[j], NT)
        own = jnp.concatenate([fluxes[i, j, :, seg(s)] for i, s in sides], axis=1)
        flux[j] = own - full_dot(solved, scaled, NT)
    n = 2 * e
    work[:, :n] = pairs[0, :n, :n] + pairs[1, :n, :n]
    factor_into(work, inverse, e)
    lower = dot3(pairs[0, n:, :n], inverse[...], NT)
    upper = dot3(pairs[1, n:, :n], inverse[...], NT)
    hint = flux[0][:, :n] + flux[1][:, :n]
    solved = full_dot(hint, inverse[...], NT)
    outs = [
        flux[0][:, n:] - full_dot(solved, lower, NT),
        flux[1][:, n:] - full_dot(solved, upper, NT),
    ]
    both[: 4 * e, : 4 * e] = pairs[0, n:, n:] - dot3(lower, lower, NT)
    both[4 * e :, 4 * e :] = pairs[1, n:, n:] - dot3(upper, upper, NT)
    cross = dot3(upper, lower, NT)
    both[4 * e :, : 4 * e] = -cross
    both[: 4 * e, 4 * e :] = -dot3(lower, upper, NT)
    radial_in = [(1 - radial_bit) * 4 + 2, (1 - radial_bit) * 4 + 3]
    radial_out = [radial_bit * 4 + 2, radial_bit * 4 + 3]
    axial_in = [1 - axial_bit, 5 - axial_bit]
    axial_out = [axial_bit, axial_bit + 4]

    def rows_of(s):
        return pl.ds(pl.multiple_of(s * e, e), e)

    def pieces(target, row_list, column_list, first):
        for p, r in enumerate(row_list):
            for q, c in enumerate(column_list):
                target[(first + p) * e : (first + p + 1) * e, seg(q)] = both[rows_of(r), rows_of(c)]

    pieces(radial, radial_in, radial_in, 0)
    pieces(rest, axial_in + axial_out + radial_out, radial_in, 0)
    pieces(axial, axial_in + axial_out + radial_out, axial_in, 0)
    final = axial_out + radial_out
    for q, order in enumerate(ORDERS):

        @pl.when(2 * axial_bit + radial_bit == q)
        def _():
            ordered = [final[o] for o in order]
            pieces(outer, ordered, ordered, 0)

    def chosen(flag, one, nought):
        return jnp.where(flag == 1, one, nought)

    zero, one = outs
    low = jnp.concatenate([zero[:, seg(0)], one[:, seg(0)]], axis=1)
    high = jnp.concatenate([zero[:, seg(1)], one[:, seg(1)]], axis=1)
    radial[2 * e : 2 * e + 1, :] = chosen(radial_bit, zero[:, 2 * e :], one[:, 2 * e :])
    radial[2 * e + 1 : 2 * e + 2, :] = chosen(axial_bit, low, high)
    radial[2 * e + 2 : 2 * e + 3, :] = chosen(axial_bit, high, low)
    radial[2 * e + 3 : 2 * e + 4, :] = chosen(radial_bit, one[:, 2 * e :], zero[:, 2 * e :])
    radial[2 * e + 4 :, :] = jnp.zeros((4, 2 * e), F32)


def factor_kernel(one, two, inverse, solved, work):
    n = inverse.shape[0]
    work[:, :n] = one[:n, :] + two[:n, :]
    factor_into(work, inverse, 128)
    hint = one[n : n + 1, :] + two[n : n + 1, :]
    solved[...] = full_dot(hint, inverse[...], NT)


def first_kernel(
    inverse, solved, radial, radial_far, rest, rest_far, axial, axial_far,
    schur, outer, scaled, remaining,
):
    n = inverse.shape[0]
    own = dot3(rest[...], inverse[...], NT)
    far = dot3(rest_far[...], inverse[...], NT)
    scaled[0] = own[n:, :]
    scaled[1] = far[n:, :]
    own_in, far_in = own[:n, :], far[:n, :]
    parts = ((axial[...], own), (-dot3(own, far_in, NT), own), (-dot3(far, own_in, NT), far))
    near = axial[...] - dot3(own, own_in, NT)
    opposite = axial_far[...] - dot3(far, far_in, NT)
    schur[:n, :n] = near[:n, :]
    schur[:n, n:] = parts[1][0][:n, :]
    schur[n : 2 * n, :n] = parts[2][0][:n, :]
    schur[n : 2 * n, n:] = opposite[:n, :]
    outer[: 2 * n, :n] = near[n:, :]
    outer[: 2 * n, n:] = parts[1][0][n:, :]
    outer[2 * n :, :n] = parts[2][0][n:, :]
    outer[2 * n :, n:] = opposite[n:, :]
    own_flux = full_dot(solved[...], own, NT)
    far_flux = full_dot(solved[...], far_in, NT)
    schur[2 * n : 2 * n + 1, :n] = radial[n + 1 : n + 2, :] - own_flux[:, :n]
    schur[2 * n : 2 * n + 1, n:] = radial_far[n + 1 : n + 2, :] - far_flux
    schur[2 * n + 1 :, :] = jnp.zeros((7, 2 * n), F32)
    remaining[:, :n] = radial[n + 2 : n + 3, :] - own_flux[:, n : 2 * n]
    remaining[:, n:] = radial[n + 3 : n + 4, :] - own_flux[:, 2 * n :]


def last_kernel(
    inverse, solved, outer, outer_far, scaled, remaining, own_map, merged, merged_flux, rows, mine
):
    n = inverse.shape[0]
    e = n // 4
    axial_bit, radial_bit = halves()
    quarter = 2 * axial_bit + radial_bit

    @pl.loop(0, 4)
    def _(slot):
        start = pl.multiple_of(lax.rem(slot, 2) * n, n)

        @pl.when(slot < 2)
        def _():
            rows[slot, :, :n] = dot3(outer[pl.ds(start, n), :], inverse[...], NT)
            rows[slot, :, n:] = scaled[slot]

        @pl.when(slot >= 2)
        def _():
            rows[slot, :, :n] = dot3(outer_far[pl.ds(start, n), :], inverse[...], NT)
            rows[slot, :, n:] = jnp.zeros((n, n // 2), F32)

    flux = remaining[...] - full_dot(solved[...], rows[0, :, :n], NT)
    for q, order in enumerate(ORDERS):

        @pl.when(quarter == q)
        def _():
            for p, o in enumerate(order):
                mine[p * e : (p + 1) * e, :] = rows[0, o * e : (o + 1) * e, :]
                merged_flux[:, p * e : (p + 1) * e] = flux[:, o * e : (o + 1) * e]

    for q, order in enumerate(ORDERS):
        slot = (axial_bit + q // 2) % 2 * 2 + (radial_bit + q % 2) % 2
        taken = jnp.concatenate([rows[slot, o * e : (o + 1) * e, :] for o in order], axis=0)
        product = dot3(mine[...], taken, NT)
        merged[:, q * n : (q + 1) * n] = jnp.where(quarter == q, own_map[...], 0.0) - product


def shards(leaf_maps, leaf_fluxes):
    e = leaf_maps.shape[2] // 4
    n = 2 * e
    radial, rest, axial, own_map = call(
        local_kernel,
        [(n + 8, n), (3 * n, n), (3 * n, n), (2 * n, 2 * n)],
        [(6 * e, e), (2, 6 * e, 6 * e), (n, 2 * n), (n, n), (8 * e, 8 * e)],
        10**9,
        leaf_maps,
        leaf_fluxes[:, :, None, :],
    )
    radial_far = swapped(radial, "rad")
    rest_far = swapped(rest, "rad")
    axial_far = swapped(axial, "rad")
    inverse, solved = call(
        factor_kernel, [(n, n), (1, n)], [(n, 2 * n)], 4 * 10**9, radial, radial_far
    )
    schur, outer, scaled, remaining = call(
        first_kernel,
        [(2 * n + 8, 2 * n), (4 * n, 2 * n), (2, 2 * n, n), (1, 2 * n)],
        [],
        10**9,
        inverse, solved, radial, radial_far, rest, rest_far, axial, axial_far,
    )
    schur_far = swapped(schur, "ax")
    outer_far = swapped(outer, "ax")
    inverse, solved = call(
        factor_kernel,
        [(2 * n, 2 * n), (1, 2 * n)],
        [(2 * n, 4 * n)],
        8 * 10**9,
        schur,
        schur_far,
    )
    merged, merged_flux = call(
        last_kernel,
        [(2 * n, 8 * n), (1, 2 * n)],
        [(4, 2 * n, 3 * n), (2 * n, 3 * n)],
        10**9,
        inverse, solved, outer, outer_far, scaled, remaining, own_map,
    )
    return merged[None, None], merged_flux[None]


def solution(mesh):
    in_specs = (P("ax", "rad", None, None), P("ax", "rad", None))
    out_specs = (P("ax", "rad", None, None), P("ax", "rad", None))
    return jax.shard_map(shards, mesh=mesh, in_specs=in_specs, out_specs=out_specs, check_vma=False)
```

time: 903 us -> 310 us (0.34); the launches traced: 892 us -> 310 us
  other arithmetic: 301 us -> 0 us
  waiting for transfers between devices: 344 us -> 145 us
  Pallas kernels: 0 us -> 150 us
  local copies, waits for them, and re-layouts: 139 us -> 5.5 us
  matrix products: 63.8 us -> 0 us
  loops' own time: 22.7 us -> 0 us
    another operation x51 -> x0, other arithmetic: 282 us -> none  [the longest x34 176 us: eliminate(): factor = jnp.linalg.cholesky(schur_block)]
    ppermute x4 -> x5, waiting for transfers between devices: 344 us -> 145 us  [swapped(): return lax.ppermute(value, axis, pairs)]
    pallas_call x0 -> x5, Pallas kernels: none -> 150 us  [call(): pl.pallas_call(kernel, out_shape=[jax.ShapeDtypeStruct(s, F32) for s in s...]
    another operation x41 -> x0, local copies, waits for them, and re-layouts: 59.5 us -> none
    cond x36 -> x0, local copies, waits for them, and re-layouts: 36.4 us -> none
    another operation x40 -> x0, matrix products: 36.4 us -> none  [the longest x15 20.4 us: eliminate(): lax.linalg.triangular_solve(factor, coupling, left_side=False, lower=True...]
    dot_general x10 -> x0, matrix products: 27.4 us -> none  [the longest x4 17.5 us: dense_merge(): jnp.dot(scaled_rows, scaled_rows.T, precision=lax.Precision.HIGHEST)]
    another operation x8 -> x0, loops' own time: 22.7 us -> none  [the longest x1 12.5 us: finish_second(): lax.cond(axial_bit == 0, lambda: eliminate_columns(own_cols, far_cols, hi...]
  transfers between devices with their start and end apart: 4 -> 5, of which waited for: 2 -> 2; matrix products, arithmetic and copies ran while one was open for 4% -> 0% of each run, Pallas kernels for 0% -> 26%
where the time goes in v1:
time: 310 us
  Pallas kernels  150 us (48%)
  waiting for transfers between devices  145 us (47%)
  starting transfers between devices  9 us (3%)
  local copies, waits for them, and re-layouts  5.5 us (2%)
    pallas_call x5, Pallas kernels, call(): pl.pallas_call(kernel, out_shape=[jax.ShapeDtypeStruct(s, F32) for s in s...  150 us
    ppermute x5, waiting for transfers between devices, swapped(): return lax.ppermute(value, axis, pairs)  145 us
    ppermute x5, starting transfers between devices, swapped(): return lax.ppermute(value, axis, pairs)  9 us
  transfers between devices with their start and end apart: 5, of which 2 were waited for; matrix products, arithmetic and copies ran while one was open for 0% of the time, Pallas kernels for 26%

profile of v1, /device:TPU:0, one launch (start us, length us, event | category | flops | bytes accessed | tf_op | source)
XLA Modules:
  0.0 310.0 jit_solution(13038719736513467895)
XLA Ops:
  0.6 1.3 broadcast_in_dim.9.fluxes
  1.9 47.4 %shard_map.41 = (f32[264,256]{1,0:T(8,128)}, f32[768,256]{1,0:T(8,128)}, f32[768,256]{1,0:T(8,128)}, f32[512,512]{1,0:T(8,128)}) custom-call(f32[2,2,512,512]{3,2,1,0:T(8,128)} %maps.1, f32[2,2,1,512]{3,2,1,0:T(1,128)} %broadcast_in_dim.9.fluxes), custom_call_target="tpu_custom_call" | custom-call | flops 1000000000 | bytes 8404992 | tf_op jit(solution)/shard_map/pallas_call | solution.py:101
  49.3 4.0 %collective-permute-start.1 = (f32[768,256]{1,0:T(8,128)}, f32[768,256]{1,0:T(8,128)S(1)}, u32[]{:S(2)}, u32[]{:S(2)}) collective-permute-start(f32[768,256]{1,0:T(8,128)} %get-tuple-element.19.rest), channel_id=1, source_target_pairs={{0,2},{1,3},{2,0},{3,1},{4,6},{5,7},{6,4},{7,5},{8,10},{9,11},{10,... | collective-permute-start | bytes 2359304 | tf_op jit(solution)/shard_map/ppermute | solution.py:20
  53.4 0.0 collective-permute-start.2
  53.4 2.9 collective-permute-start
  56.3 77.0 %collective-permute-done.two.radial_far = f32[264,256]{1,0:T(8,128)S(1)} collective-permute-done((f32[264,256]{1,0:T(8,128)}, f32[264,256]{1,0:T(8,128)S(1)}, u32[]{:S(2)}, u32[]{:S(2)}) %collective-permute-start) | collective-permute-done | bytes 270368 | tf_op jit(solution)/shard_map/ppermute | solution.py:20
  133.3 0.0 copy-start.3
  133.3 0.7 copy-done.3
  134.0 25.7 %shard_map.42 = (f32[256,256]{1,0:T(8,128)}, f32[1,256]{1,0:T(1,128)}) custom-call(f32[264,256]{1,0:T(8,128)} %get-tuple-element.16.one.radial, f32[264,256]{1,0:T(8,128)} %copy-done.3), custom_call_target="tpu_custom_call" | custom-call | flops 4000000000 | bytes 1081344 | tf_op jit(solution)/shard_map/pallas_call | solution.py:101
  159.6 0.0 collective-permute-done.1.rest_far
  159.6 0.0 copy-start.1
  159.7 0.0 collective-permute-done.2.axial_far
  159.7 0.0 copy-start.2
  159.7 0.9 copy-done.1
  160.5 0.3 copy-done.2
  160.8 6.2 %shard_map.43 = (f32[520,512]{1,0:T(8,128)}, f32[1024,512]{1,0:T(8,128)}, f32[2,512,256]{2,1,0:T(8,128)}, f32[1,512]{1,0:T(1,128)}) custom-call(f32[256,256]{1,0:T(8,128)} %get-tuple-element.17.inverse, f32[1,256]{1,0:T(1,128)} %get-tuple-element.18.solved, f32[264,256]{1,0:T(8,128)} %get-tuple-element.16.one.radial, f32[264,256]{1,0:T(8,128)} %copy-done.3, ...), custom_call_target="tpu_custom_call" | custom-call | flops 1000000000 | bytes 7899136 | tf_op jit(solution)/shard_map/pallas_call | solution.py:101
  167.0 1.6 collective-permute-start.4
  168.5 0.5 collective-permute-start.3
  169.0 67.8 %collective-permute-done.3.two = f32[520,512]{1,0:T(8,128)S(1)} collective-permute-done((f32[520,512]{1,0:T(8,128)}, f32[520,512]{1,0:T(8,128)S(1)}, u32[]{:S(2)}, u32[]{:S(2)}) %collective-permute-start.3) | collective-permute-done | bytes 1064992 | tf_op jit(solution)/shard_map/ppermute | solution.py:20
  236.8 1.0 copy-done.4
  237.9 55.4 %shard_map.44 = (f32[512,512]{1,0:T(8,128)}, f32[1,512]{1,0:T(1,128)}) custom-call(f32[520,512]{1,0:T(8,128)} %get-tuple-element.21.one, f32[520,512]{1,0:T(8,128)} %copy-done.4), custom_call_target="tpu_custom_call" | custom-call | flops 8000000000 | bytes 4259840 | tf_op jit(solution)/shard_map/pallas_call | solution.py:101
  293.3 0.0 collective-permute-done.4.outer_far
  293.3 1.3 copy-done
  294.6 15.3 %shard_map.45 = (f32[512,2048]{1,0:T(8,128)}, f32[1,512]{1,0:T(1,128)}) custom-call(f32[512,512]{1,0:T(8,128)} %get-tuple-element.22.inverse, f32[1,512]{1,0:T(1,128)} %get-tuple-element.23.solved, f32[1024,512]{1,0:T(8,128)} %get-tuple-element.24.outer, f32[1024,512]{1,0:T(8,128)} %copy-done, f32[2,512,256]{2,1,0:T(8,128)} %get-tuple-element.25.scaled, ...), custom_call_target="tpu_custom_call" | custom-call | flops 1000000000 | bytes 14688256 | tf_op jit(solution)/shard_map/pallas_call | solution.py:101
  (2 shorter events, 0.0 us)
Async XLA Ops:
  49.3 110.3 %collective-permute-start.1 = (f32[768,256]{1,0:T(8,128)}, f32[768,256]{1,0:T(8,128)S(1)}, u32[]{:S(2)}, u32[]{:S(2)}) collective-permute-start(f32[768,256]{1,0:T(8,128)} %get-tuple-element.19.rest), channel_id=1, source_target_pairs={{0,2},{1,3},{2,0},{3,1},{4,6},{5,7},{6,4},{7,5},{8,10},{9,11},{10,... | collective-permute-start | bytes 2359304 | tf_op jit(solution)/shard_map/ppermute | solution.py:20
  53.4 106.3 %collective-permute-start.2 = (f32[768,256]{1,0:T(8,128)}, f32[768,256]{1,0:T(8,128)S(1)}, u32[]{:S(2)}, u32[]{:S(2)}) collective-permute-start(f32[768,256]{1,0:T(8,128)} %get-tuple-element.20.axial), channel_id=1, source_target_pairs={{0,2},{1,3},{2,0},{3,1},{4,6},{5,7},{6,4},{7,5},{8,10},{9,11},{10,... | collective-permute-start | bytes 2359304 | tf_op jit(solution)/shard_map/ppermute | solution.py:20
  53.4 79.9 %collective-permute-start = (f32[264,256]{1,0:T(8,128)}, f32[264,256]{1,0:T(8,128)S(1)}, u32[]{:S(2)}, u32[]{:S(2)}) collective-permute-start(f32[264,256]{1,0:T(8,128)} %get-tuple-element.16.one.radial), channel_id=1, source_target_pairs={{0,2},{1,3},{2,0},{3,1},{4,6},{5,7},{6,4},{7,5},{8,10},{9,11},{10,... | collective-permute-start | bytes 811016 | tf_op jit(solution)/shard_map/ppermute | solution.py:20
  133.3 0.7 copy-start.3
  159.6 0.9 copy-start.1
  159.7 1.1 copy-start.2
  167.0 126.3 %collective-permute-start.4 = (f32[1024,512]{1,0:T(8,128)}, f32[1024,512]{1,0:T(8,128)S(1)}, u32[]{:S(2)}, u32[]{:S(2)}) collective-permute-start(f32[1024,512]{1,0:T(8,128)} %get-tuple-element.24.outer), channel_id=1, source_target_pairs={{0,16},{4,20},{8,24},{12,28},{16,0},{20,4},{24,8},{28,12},{1,17},{... | collective-permute-start | bytes 6291464 | tf_op jit(solution)/shard_map/ppermute | solution.py:20
  168.5 68.3 %collective-permute-start.3 = (f32[520,512]{1,0:T(8,128)}, f32[520,512]{1,0:T(8,128)S(1)}, u32[]{:S(2)}, u32[]{:S(2)}) collective-permute-start(f32[520,512]{1,0:T(8,128)} %get-tuple-element.21.one), channel_id=1, source_target_pairs={{0,16},{4,20},{8,24},{12,28},{16,0},{20,4},{24,8},{28,12},{1,17},{... | collective-permute-start | bytes 3194888 | tf_op jit(solution)/shard_map/ppermute | solution.py:20
  236.8 1.0 copy-start.4
  293.3 1.4 copy-start

commit v2 on v1

--- a/solution.py
+++ b/solution.py
@@ -49,34 +49,54 @@
 def invert_factors(tiles):
     size = tiles[0].shape[0]
     count = size // 8
-    lane = lax.broadcasted_iota(jnp.int32, (1, size), 1)
-    sub = lax.broadcasted_iota(jnp.int32, (8, 1), 0)
+    lane = lax.broadcasted_iota(jnp.int32, (8, size), 1)
+    sub = lax.broadcasted_iota(jnp.int32, (8, size), 0)
+
+    def spread(row):
+        return jnp.broadcast_to(row, (8, size))
+
     works = [[t[8 * i : 8 * i + 8, :] for i in range(count)] for t in tiles]
-    for k in range(size):
-        t0, s0 = k // 8, k % 8
-        here = lane == k
-        for work in works:
-            row = work[t0][s0 : s0 + 1, :]
-            inverse = 1.0 / work[t0][s0 : s0 + 1, k : k + 1]
-            scaled = jnp.where(here, 1.0, row) * inverse
-            for t in range(t0, count):
-                if t == t0 and s0 == 7:
-                    continue
+    scales = [[None] * count for _ in tiles]
+    for t0 in range(count):
+        first = 8 * t0
+        inside = (lane >= first) & (lane < first + 8)
+        for work, scale in zip(works, scales):
+            part = work[t0]
+            columns = [spread(part[:, first + c : first + c + 1]) for c in range(8)]
+            part = jnp.where(inside, (lane == sub + first).astype(F32), part)
+            pivots = columns[0]
+            rows, factors = [], []
+            for s in range(8):
+                if s:
+                    pivots = jnp.where(sub >= s, columns[s], pivots)
+                inverse = 1.0 / spread(columns[s][s : s + 1, :])
+                rows.append(spread(part[s : s + 1, :]) * inverse)
+                factors.append([spread(columns[c][s : s + 1, :]) * inverse for c in range(s + 1, 8)])
+                lower = jnp.where(sub > s, columns[s], 0.0)
+                part = part - lower * rows[s]
+                for c in range(s + 1, 8):
+                    columns[c] = columns[c] - lower * factors[s][c - s - 1]
+            work[t0] = part
+            scale[t0] = pivots
+            for t in range(t0 + 1, count):
                 part = work[t]
-                column = part[:, k : k + 1]
-                fresh = jnp.where(here, 0.0, part) - column * scaled
-                if t == t0:
-                    fresh = jnp.where(sub > s0, fresh, part)
-                work[t] = fresh
-    results = []
-    lanes = lax.broadcasted_iota(jnp.int32, (size, size), 1)
-    rows = lax.broadcasted_iota(jnp.int32, (size, size), 0)
-    for work in works:
-        whole = jnp.concatenate(work, axis=0)
-        pivots = jnp.sum(jnp.where(lanes == rows, whole, 0.0), axis=1, keepdims=True)
-        unit = jnp.where(lanes < rows, whole, jnp.where(lanes == rows, 1.0, 0.0))
-        results.append(unit * lax.rsqrt(pivots))
-    return results
+                columns = [spread(part[:, first + c : first + c + 1]) for c in range(8)]
+                part = jnp.where(inside, 0.0, part)
+                for s in range(8):
+                    part = part - columns[s] * rows[s]
+                    for c in range(s + 1, 8):
+                        columns[c] = columns[c] - columns[s] * factors[s][c - s - 1]
+                work[t] = part
+    return [
+        jnp.concatenate(
+            [
+                jnp.where(lane <= sub + 8 * i, work[i], 0.0) * lax.rsqrt(scale[i])
+                for i in range(count)
+            ],
+            axis=0,
+        )
+        for work, scale in zip(works, scales)
+    ]
 
 
 def factor_into(work, out, step):
@@ -89,11 +109,11 @@
     def _(b):
         start = pl.multiple_of(b * step, step)
         inverse = invert_factors([work[pl.ds(start, step), pl.ds(start, step)]])[0]
-        panel = full_dot(inverse, work[pl.ds(start, step), :], NN)
+        panel = dot3(inverse, work[pl.ds(start, step), :], NN)
         out[pl.ds(start, step), :] = panel[:, n:]
         lanes = lax.broadcasted_iota(jnp.int32, (step, n), 1)
         tail = jnp.where(lanes >= start + step, panel[:, :n], 0.0)
-        work[...] -= full_dot(tail, panel, TN)
+        work[...] -= dot3(tail, panel, TN)
 
 
 def call(kernel, shapes, scratch, flops, *args):
@@ -280,8 +300,9 @@
         leaf_fluxes[:, :, None, :],
     )
     radial_far = swapped(radial, "rad")
-    rest_far = swapped(rest, "rad")
-    axial_far = swapped(axial, "rad")
+    radial_far, rest_late, axial_late = lax.optimization_barrier((radial_far, rest, axial))
+    rest_far = swapped(rest_late, "rad")
+    axial_far = swapped(axial_late, "rad")
     inverse, solved = call(
         factor_kernel, [(n, n), (1, n)], [(n, 2 * n)], 4 * 10**9, radial, radial_far
     )
@@ -293,7 +314,8 @@
         inverse, solved, radial, radial_far, rest, rest_far, axial, axial_far,
     )
     schur_far = swapped(schur, "ax")
-    outer_far = swapped(outer, "ax")
+    schur_far, outer_late = lax.optimization_barrier((schur_far, outer))
+    outer_far = swapped(outer_late, "ax")
     inverse, solved = call(
         factor_kernel,
         [(2 * n, 2 * n), (1, 2 * n)],

time: 310 us -> 210 us (0.68)
  Pallas kernels: 150 us -> 85 us
  waiting for transfers between devices: 145 us -> 111 us
    pallas_call x5, Pallas kernels: 150 us -> 85 us  [call(): pl.pallas_call(kernel, out_shape=[jax.ShapeDtypeStruct(s, F32) for s in s...]
    ppermute x5, waiting for transfers between devices: 145 us -> 111 us  [swapped(): return lax.ppermute(value, axis, pairs)]
  transfers between devices with their start and end apart: 5 -> 5, of which waited for: 2 -> 5; matrix products, arithmetic and copies ran while one was open for 0% -> 0% of each run, Pallas kernels for 26% -> 17%
where the time goes in v2:
time: 210 us
  waiting for transfers between devices  111 us (53%)
  Pallas kernels  85 us (40%)
  starting transfers between devices  9.24 us (4%)
  local copies, waits for them, and re-layouts  3.56 us (2%)
    ppermute x5, waiting for transfers between devices, swapped(): return lax.ppermute(value, axis, pairs)  111 us
    pallas_call x5, Pallas kernels, call(): pl.pallas_call(kernel, out_shape=[jax.ShapeDtypeStruct(s, F32) for s in s...  85 us
    ppermute x5, starting transfers between devices, swapped(): return lax.ppermute(value, axis, pairs)  9.24 us
  transfers between devices with their start and end apart: 5, of which 5 were waited for; matrix products, arithmetic and copies ran while one was open for 0% of the time, Pallas kernels for 17%

profile of v2, /device:TPU:0, one launch (start us, length us, event | category | flops | bytes accessed | tf_op | source)
XLA Modules:
  0.0 209.5 jit_solution(1575453973961793310)
XLA Ops:
  0.6 1.3 broadcast_in_dim.9.fluxes
  1.9 27.5 %shard_map.41 = (f32[264,256]{1,0:T(8,128)}, f32[768,256]{1,0:T(8,128)}, f32[768,256]{1,0:T(8,128)}, f32[512,512]{1,0:T(8,128)}) custom-call(f32[2,2,512,512]{3,2,1,0:T(8,128)} %maps.1, f32[2,2,1,512]{3,2,1,0:T(1,128)} %broadcast_in_dim.9.fluxes), custom_call_target="tpu_custom_call" | custom-call | flops 1000000000 | bytes 8404992 | tf_op jit(solution)/shard_map/pallas_call | solution.py:121
  29.4 4.1 %collective-permute-start = (f32[264,256]{1,0:T(8,128)}, f32[264,256]{1,0:T(8,128)S(1)}, u32[]{:S(2)}, u32[]{:S(2)}) collective-permute-start(f32[264,256]{1,0:T(8,128)} %get-tuple-element.21.one.radial), channel_id=1, source_target_pairs={{0,2},{1,3},{2,0},{3,1},{4,6},{5,7},{6,4},{7,5},{8,10},{9,11},{10,... | collective-permute-start | bytes 811016 | tf_op jit(solution)/shard_map/ppermute | solution.py:20
  33.5 12.5 %collective-permute-done.two.radial_far = f32[264,256]{1,0:T(8,128)S(1)} collective-permute-done((f32[264,256]{1,0:T(8,128)}, f32[264,256]{1,0:T(8,128)S(1)}, u32[]{:S(2)}, u32[]{:S(2)}) %collective-permute-start) | collective-permute-done | bytes 270368 | tf_op jit(solution)/shard_map/ppermute | solution.py:20
  45.9 0.0 copy-start.3
  45.9 0.0 collective-permute-start.1
  45.9 2.9 %collective-permute-start.2 = (f32[768,256]{1,0:T(8,128)}, f32[768,256]{1,0:T(8,128)S(1)}, u32[]{:S(2)}, u32[]{:S(2)}) collective-permute-start(f32[768,256]{1,0:T(8,128)} %get-tuple-element.28.axial), channel_id=1, source_target_pairs={{0,2},{1,3},{2,0},{3,1},{4,6},{5,7},{6,4},{7,5},{8,10},{9,11},{10,... | collective-permute-start | bytes 2359304 | tf_op jit(solution)/shard_map/ppermute | solution.py:20
  48.9 0.0 copy-done.3
  48.9 11.3 %shard_map.42 = (f32[256,256]{1,0:T(8,128)}, f32[1,256]{1,0:T(1,128)}) custom-call(f32[264,256]{1,0:T(8,128)} %get-tuple-element.21.one.radial, f32[264,256]{1,0:T(8,128)} %copy-done.3), custom_call_target="tpu_custom_call" | custom-call | flops 4000000000 | bytes 1081344 | tf_op jit(solution)/shard_map/pallas_call | solution.py:121
  60.2 41.0 %collective-permute-done.1.rest_far = f32[768,256]{1,0:T(8,128)S(1)} collective-permute-done((f32[768,256]{1,0:T(8,128)}, f32[768,256]{1,0:T(8,128)S(1)}, u32[]{:S(2)}, u32[]{:S(2)}) %collective-permute-start.1) | collective-permute-done | bytes 786464 | tf_op jit(solution)/shard_map/ppermute | solution.py:20
  101.2 0.0 copy-start.1
  101.2 15.1 %collective-permute-done.2.axial_far = f32[768,256]{1,0:T(8,128)S(1)} collective-permute-done((f32[768,256]{1,0:T(8,128)}, f32[768,256]{1,0:T(8,128)S(1)}, u32[]{:S(2)}, u32[]{:S(2)}) %collective-permute-start.2) | collective-permute-done | bytes 786464 | tf_op jit(solution)/shard_map/ppermute | solution.py:20
  116.3 0.0 copy-start.2
  116.3 0.0 copy-done.1
  116.3 0.9 copy-done.2
  117.2 6.2 %shard_map.43 = (f32[520,512]{1,0:T(8,128)}, f32[1024,512]{1,0:T(8,128)}, f32[2,512,256]{2,1,0:T(8,128)}, f32[1,512]{1,0:T(1,128)}) custom-call(f32[256,256]{1,0:T(8,128)} %get-tuple-element.25.inverse, f32[1,256]{1,0:T(1,128)} %get-tuple-element.26.solved, f32[264,256]{1,0:T(8,128)} %get-tuple-element.21.one.radial, f32[264,256]{1,0:T(8,128)} %copy-done.3, ...), custom_call_target="tpu_custom_call" | custom-call | flops 1000000000 | bytes 7899136 | tf_op jit(solution)/shard_map/pallas_call | solution.py:121
  123.4 1.3 collective-permute-start.3
  124.7 22.7 %collective-permute-done.3.two = f32[520,512]{1,0:T(8,128)S(1)} collective-permute-done((f32[520,512]{1,0:T(8,128)}, f32[520,512]{1,0:T(8,128)S(1)}, u32[]{:S(2)}, u32[]{:S(2)}) %collective-permute-start.3) | collective-permute-done | bytes 1064992 | tf_op jit(solution)/shard_map/ppermute | solution.py:20
  147.4 1.0 collective-permute-start.4
  148.4 0.0 copy-done.4
  148.4 24.4 %shard_map.44 = (f32[512,512]{1,0:T(8,128)}, f32[1,512]{1,0:T(1,128)}) custom-call(f32[520,512]{1,0:T(8,128)} %get-tuple-element.29.one, f32[520,512]{1,0:T(8,128)} %copy-done.4), custom_call_target="tpu_custom_call" | custom-call | flops 8000000000 | bytes 4259840 | tf_op jit(solution)/shard_map/pallas_call | solution.py:121
  172.8 19.8 %collective-permute-done.4.outer_far = f32[1024,512]{1,0:T(8,128)S(1)} collective-permute-done((f32[1024,512]{1,0:T(8,128)}, f32[1024,512]{1,0:T(8,128)S(1)}, u32[]{:S(2)}, u32[]{:S(2)}) %collective-permute-start.4) | collective-permute-done | bytes 2097184 | tf_op jit(solution)/shard_map/ppermute | solution.py:20
  192.6 1.3 copy-done
  193.9 15.6 %shard_map.45 = (f32[512,2048]{1,0:T(8,128)}, f32[1,512]{1,0:T(1,128)}) custom-call(f32[512,512]{1,0:T(8,128)} %get-tuple-element.32.inverse, f32[1,512]{1,0:T(1,128)} %get-tuple-element.33.solved, f32[1024,512]{1,0:T(8,128)} %get-tuple-element.34.outer, f32[1024,512]{1,0:T(8,128)} %copy-done, f32[2,512,256]{2,1,0:T(8,128)} %get-tuple-element.35.scaled, ...), custom_call_target="tpu_custom_call" | custom-call | flops 1000000000 | bytes 14688256 | tf_op jit(solution)/shard_map/pallas_call | solution.py:121
  (2 shorter events, 0.0 us)
Async XLA Ops:
  29.4 16.5 %collective-permute-start = (f32[264,256]{1,0:T(8,128)}, f32[264,256]{1,0:T(8,128)S(1)}, u32[]{:S(2)}, u32[]{:S(2)}) collective-permute-start(f32[264,256]{1,0:T(8,128)} %get-tuple-element.21.one.radial), channel_id=1, source_target_pairs={{0,2},{1,3},{2,0},{3,1},{4,6},{5,7},{6,4},{7,5},{8,10},{9,11},{10,... | collective-permute-start | bytes 811016 | tf_op jit(solution)/shard_map/ppermute | solution.py:20
  45.9 2.9 %copy-start.3 = (f32[264,256]{1,0:T(8,128)}, f32[264,256]{1,0:T(8,128)S(1)}, u32[]{:S(2)}) copy-start(f32[264,256]{1,0:T(8,128)S(1)} %collective-permute-done.two.radial_far) | copy-start | bytes 811012
  45.9 55.3 %collective-permute-start.1 = (f32[768,256]{1,0:T(8,128)}, f32[768,256]{1,0:T(8,128)S(1)}, u32[]{:S(2)}, u32[]{:S(2)}) collective-permute-start(f32[768,256]{1,0:T(8,128)} %get-tuple-element.27.rest), channel_id=1, source_target_pairs={{0,2},{1,3},{2,0},{3,1},{4,6},{5,7},{6,4},{7,5},{8,10},{9,11},{10,... | collective-permute-start | bytes 2359304 | tf_op jit(solution)/shard_map/ppermute | solution.py:20
  45.9 70.4 %collective-permute-start.2 = (f32[768,256]{1,0:T(8,128)}, f32[768,256]{1,0:T(8,128)S(1)}, u32[]{:S(2)}, u32[]{:S(2)}) collective-permute-start(f32[768,256]{1,0:T(8,128)} %get-tuple-element.28.axial), channel_id=1, source_target_pairs={{0,2},{1,3},{2,0},{3,1},{4,6},{5,7},{6,4},{7,5},{8,10},{9,11},{10,... | collective-permute-start | bytes 2359304 | tf_op jit(solution)/shard_map/ppermute | solution.py:20
  101.2 15.1 %copy-start.1 = (f32[768,256]{1,0:T(8,128)}, f32[768,256]{1,0:T(8,128)S(1)}, u32[]{:S(2)}) copy-start(f32[768,256]{1,0:T(8,128)S(1)} %collective-permute-done.1.rest_far) | copy-start | bytes 2359300
  116.3 0.9 copy-start.2
  123.4 24.0 %collective-permute-start.3 = (f32[520,512]{1,0:T(8,128)}, f32[520,512]{1,0:T(8,128)S(1)}, u32[]{:S(2)}, u32[]{:S(2)}) collective-permute-start(f32[520,512]{1,0:T(8,128)} %get-tuple-element.29.one), channel_id=1, source_target_pairs={{0,16},{4,20},{8,24},{12,28},{16,0},{20,4},{24,8},{28,12},{1,17},{... | collective-permute-start | bytes 3194888 | tf_op jit(solution)/shard_map/ppermute | solution.py:20
  147.4 1.0 copy-start.4
  147.4 45.2 %collective-permute-start.4 = (f32[1024,512]{1,0:T(8,128)}, f32[1024,512]{1,0:T(8,128)S(1)}, u32[]{:S(2)}, u32[]{:S(2)}) collective-permute-start(f32[1024,512]{1,0:T(8,128)} %get-tuple-element.34.outer), channel_id=1, source_target_pairs={{0,16},{4,20},{8,24},{12,28},{16,0},{20,4},{24,8},{28,12},{1,17},{... | collective-permute-start | bytes 6291464 | tf_op jit(solution)/shard_map/ppermute | solution.py:20
  192.6 1.4 copy-start

commit v3 on v2

--- a/solution.py
+++ b/solution.py
@@ -131,7 +131,9 @@
     )(*args)
 
 
-def local_kernel(maps, fluxes, radial, rest, axial, outer, coupled, pairs, work, inverse, both):
+def local_kernel(
+    maps, fluxes, radial, rest, meet, side, outer, coupled, pairs, work, inverse, both
+):
     e = maps.shape[2] // 4
     axial_bit, radial_bit = halves()
 
@@ -190,7 +192,8 @@
 
     pieces(radial, radial_in, radial_in, 0)
     pieces(rest, axial_in + axial_out + radial_out, radial_in, 0)
-    pieces(axial, axial_in + axial_out + radial_out, axial_in, 0)
+    pieces(meet, axial_in, axial_in, 0)
+    pieces(side, axial_out + radial_out, axial_in, 0)
     final = axial_out + radial_out
     for q, order in enumerate(ORDERS):
 
@@ -221,58 +224,70 @@
 
 
 def first_kernel(
-    inverse, solved, radial, radial_far, rest, rest_far, axial, axial_far,
-    schur, outer, scaled, remaining,
+    inverse, solved, radial, radial_far, rest, rest_far, thin, scaled, remaining
 ):
     n = inverse.shape[0]
     own = dot3(rest[...], inverse[...], NT)
     far = dot3(rest_far[...], inverse[...], NT)
+    thin[:n, :] = own[:n, :]
+    thin[n : 2 * n, :] = far[:n, :]
     scaled[0] = own[n:, :]
     scaled[1] = far[n:, :]
-    own_in, far_in = own[:n, :], far[:n, :]
-    parts = ((axial[...], own), (-dot3(own, far_in, NT), own), (-dot3(far, own_in, NT), far))
-    near = axial[...] - dot3(own, own_in, NT)
-    opposite = axial_far[...] - dot3(far, far_in, NT)
-    schur[:n, :n] = near[:n, :]
-    schur[:n, n:] = parts[1][0][:n, :]
-    schur[n : 2 * n, :n] = parts[2][0][:n, :]
-    schur[n : 2 * n, n:] = opposite[:n, :]
-    outer[: 2 * n, :n] = near[n:, :]
-    outer[: 2 * n, n:] = parts[1][0][n:, :]
-    outer[2 * n :, :n] = parts[2][0][n:, :]
-    outer[2 * n :, n:] = opposite[n:, :]
     own_flux = full_dot(solved[...], own, NT)
-    far_flux = full_dot(solved[...], far_in, NT)
-    schur[2 * n : 2 * n + 1, :n] = radial[n + 1 : n + 2, :] - own_flux[:, :n]
-    schur[2 * n : 2 * n + 1, n:] = radial_far[n + 1 : n + 2, :] - far_flux
-    schur[2 * n + 1 :, :] = jnp.zeros((7, 2 * n), F32)
+    far_flux = full_dot(solved[...], far[:n, :], NT)
+    thin[2 * n : 2 * n + 1, :] = radial[n + 1 : n + 2, :] - own_flux[:, :n]
+    thin[2 * n + 1 : 2 * n + 2, :] = radial_far[n + 1 : n + 2, :] - far_flux
+    thin[2 * n + 2 :, :] = jnp.zeros((6, n), F32)
     remaining[:, :n] = radial[n + 2 : n + 3, :] - own_flux[:, n : 2 * n]
     remaining[:, n:] = radial[n + 3 : n + 4, :] - own_flux[:, 2 * n :]
 
 
+def second_factor_kernel(
+    meet, meet_far, thin, thin_far, inverse, solved, bent, bent_far, work
+):
+    m = inverse.shape[0]
+    n = m // 2
+    own, far = thin[:m, :], thin_far[:m, :]
+    work[:, :m] = -(dot3(own, own, NT) + dot3(far, far, NT))
+    work[:n, :n] += meet[...]
+    work[n:, n:m] += meet_far[...]
+    factor_into(work, inverse, 128)
+    hint = jnp.concatenate(
+        [thin[m + i : m + i + 1, :] + thin_far[m + i : m + i + 1, :] for i in range(2)], axis=1
+    )
+    solved[...] = full_dot(hint, inverse[...], NT)
+    bent[...] = dot3(inverse[...], own, NN)
+    bent_far[...] = dot3(inverse[...], far, NN)
+
+
+def rows_kernel(
+    inverse, solved, bent, bent_far, side, side_rad, side_ax, scaled, scaled_far, remaining,
+    rows, flux,
+):
+    n = bent.shape[1]
+    low, high = inverse[:, :n], inverse[:, n:]
+    rows[0] = dot3(side[...], low, NT) - dot3(scaled[0], bent[...], NT)
+    rows[1] = dot3(side_rad[...], high, NT) - dot3(scaled[1], bent[...], NT)
+    rows[2] = dot3(side_ax[...], low, NT) - dot3(scaled_far[0], bent_far[...], NT)
+    flux[...] = remaining[...] - full_dot(solved[...], rows[0], NT)
+
+
 def last_kernel(
-    inverse, solved, outer, outer_far, scaled, remaining, own_map, merged, merged_flux, rows, mine
-):
-    n = inverse.shape[0]
-    e = n // 4
+    inverse, bent_far, side_diag, scaled, scaled_far, known, flux, own_map,
+    merged, merged_flux, rows, mine,
+):
+    m = inverse.shape[0]
+    n = m // 2
+    e = n // 2
     axial_bit, radial_bit = halves()
     quarter = 2 * axial_bit + radial_bit
-
-    @pl.loop(0, 4)
-    def _(slot):
-        start = pl.multiple_of(lax.rem(slot, 2) * n, n)
-
-        @pl.when(slot < 2)
-        def _():
-            rows[slot, :, :n] = dot3(outer[pl.ds(start, n), :], inverse[...], NT)
-            rows[slot, :, n:] = scaled[slot]
-
-        @pl.when(slot >= 2)
-        def _():
-            rows[slot, :, :n] = dot3(outer_far[pl.ds(start, n), :], inverse[...], NT)
-            rows[slot, :, n:] = jnp.zeros((n, n // 2), F32)
-
-    flux = remaining[...] - full_dot(solved[...], rows[0, :, :n], NT)
+    for slot in range(3):
+        rows[slot, :, :m] = known[slot]
+    rows[3, :, :m] = dot3(side_diag[...], inverse[:, n:], NT) - dot3(
+        scaled_far[1], bent_far[...], NT
+    )
+    for slot in range(4):
+        rows[slot, :, m:] = scaled[slot] if slot < 2 else jnp.zeros((m, n), F32)
     for q, order in enumerate(ORDERS):
 
         @pl.when(quarter == q)
@@ -285,51 +300,70 @@
         slot = (axial_bit + q // 2) % 2 * 2 + (radial_bit + q % 2) % 2
         taken = jnp.concatenate([rows[slot, o * e : (o + 1) * e, :] for o in order], axis=0)
         product = dot3(mine[...], taken, NT)
-        merged[:, q * n : (q + 1) * n] = jnp.where(quarter == q, own_map[...], 0.0) - product
+        merged[:, q * m : (q + 1) * m] = jnp.where(quarter == q, own_map[...], 0.0) - product
+
+
+def after(done, value):
+    return lax.optimization_barrier((done, value))
 
 
 def shards(leaf_maps, leaf_fluxes):
     e = leaf_maps.shape[2] // 4
     n = 2 * e
-    radial, rest, axial, own_map = call(
+    m = 2 * n
+    radial, rest, meet, side, own_map = call(
         local_kernel,
-        [(n + 8, n), (3 * n, n), (3 * n, n), (2 * n, 2 * n)],
-        [(6 * e, e), (2, 6 * e, 6 * e), (n, 2 * n), (n, n), (8 * e, 8 * e)],
+        [(n + 8, n), (3 * n, n), (n, n), (m, n), (m, m)],
+        [(6 * e, e), (2, 6 * e, 6 * e), (n, m), (n, n), (8 * e, 8 * e)],
         10**9,
         leaf_maps,
         leaf_fluxes[:, :, None, :],
     )
     radial_far = swapped(radial, "rad")
-    radial_far, rest_late, axial_late = lax.optimization_barrier((radial_far, rest, axial))
+    meet_ax = swapped(meet, "ax")
+    side_ax = swapped(side, "ax")
+    radial_far, rest_late = after(radial_far, rest)
     rest_far = swapped(rest_late, "rad")
-    axial_far = swapped(axial_late, "rad")
     inverse, solved = call(
-        factor_kernel, [(n, n), (1, n)], [(n, 2 * n)], 4 * 10**9, radial, radial_far
-    )
-    schur, outer, scaled, remaining = call(
+        factor_kernel, [(n, n), (1, n)], [(n, m)], 4 * 10**9, radial, radial_far
+    )
+    meet_sum = meet + meet_ax
+    rest_far, meet_late = after(rest_far, meet_sum)
+    meet_far = swapped(meet_late, "rad")
+    thin, scaled, remaining = call(
         first_kernel,
-        [(2 * n + 8, 2 * n), (4 * n, 2 * n), (2, 2 * n, n), (1, 2 * n)],
+        [(m + 8, n), (2, m, n), (1, m)],
         [],
         10**9,
-        inverse, solved, radial, radial_far, rest, rest_far, axial, axial_far,
-    )
-    schur_far = swapped(schur, "ax")
-    schur_far, outer_late = lax.optimization_barrier((schur_far, outer))
-    outer_far = swapped(outer_late, "ax")
-    inverse, solved = call(
-        factor_kernel,
-        [(2 * n, 2 * n), (1, 2 * n)],
-        [(2 * n, 4 * n)],
+        inverse, solved, radial, radial_far, rest, rest_far,
+    )
+    thin_far = swapped(thin, "ax")
+    meet_far, side_late = after(meet_far, side)
+    side_rad = swapped(side_late, "rad")
+    thin_far, scaled_late = after(thin_far, scaled)
+    scaled_far = swapped(scaled_late, "ax")
+    inverse, solved, bent, bent_far = call(
+        second_factor_kernel,
+        [(m, m), (1, m), (m, n), (m, n)],
+        [(m, 2 * m)],
         8 * 10**9,
-        schur,
-        schur_far,
+        meet_sum, meet_far, thin, thin_far,
+    )
+    inverse, side_rad = after(inverse, side_rad)
+    side_diag = swapped(side_rad, "ax")
+    known, flux = call(
+        rows_kernel,
+        [(3, m, m), (1, m)],
+        [],
+        4 * 10**9,
+        inverse, solved, bent, bent_far, side, side_rad, side_ax, scaled, scaled_far, remaining,
     )
     merged, merged_flux = call(
         last_kernel,
-        [(2 * n, 8 * n), (1, 2 * n)],
-        [(4, 2 * n, 3 * n), (2 * n, 3 * n)],
+        [(m, 4 * m), (1, m)],
+        [(4, m, 3 * n), (m, 3 * n)],
         10**9,
-        inverse, solved, outer, outer_far, scaled, remaining, own_map,
+        inverse, bent_far, side_diag, scaled, scaled_far, known, flux, own_map,
     )
     return merged[None, None], merged_flux[None]
 

time: 210 us -> 158 us (0.75)
  waiting for transfers between devices: 111 us -> 53.1 us
  Pallas kernels: 85 us -> 88.7 us
    ppermute x5 -> x9, waiting for transfers between devices: 111 us -> 53.1 us  [swapped(): return lax.ppermute(value, axis, pairs)]
    pallas_call x5 -> x6, Pallas kernels: 85 us -> 88.7 us  [call(): pl.pallas_call(kernel, out_shape=[jax.ShapeDtypeStruct(s, F32) for s in s...]
    ppermute x5 -> x9, starting transfers between devices: 9.24 us -> 9.91 us  [swapped(): return lax.ppermute(value, axis, pairs)]
  transfers between devices with their start and end apart: 5 -> 9, of which waited for: 5 -> 5; matrix products, arithmetic and copies ran while one was open for 0% -> 1% of each run, Pallas kernels for 17% -> 29%
where the time goes in v3:
time: 158 us
  Pallas kernels  88.7 us (56%)
  waiting for transfers between devices  53.1 us (34%)
  starting transfers between devices  9.91 us (6%)
  local copies, waits for them, and re-layouts  4.84 us (3%)
    pallas_call x6, Pallas kernels, call(): pl.pallas_call(kernel, out_shape=[jax.ShapeDtypeStruct(s, F32) for s in s...  88.7 us
    ppermute x9, waiting for transfers between devices, swapped(): return lax.ppermute(value, axis, pairs)  53.1 us
    ppermute x9, starting transfers between devices, swapped(): return lax.ppermute(value, axis, pairs)  9.91 us
    unnamed x20, local copies, waits for them, and re-layouts  3.54 us
  transfers between devices with their start and end apart: 9, of which 5 were waited for; matrix products, arithmetic and copies ran while one was open for 1% of the time, Pallas kernels for 29%

profile of v3, /device:TPU:0, one launch (start us, length us, event | category | flops | bytes accessed | tf_op | source)
XLA Modules:
  0.0 158.2 jit_solution(5421259863259770540)
XLA Ops:
  0.6 1.3 broadcast_in_dim.9.fluxes
  1.9 27.4 %shard_map.41 = (f32[264,256]{1,0:T(8,128)}, f32[768,256]{1,0:T(8,128)}, f32[256,256]{1,0:T(8,128)}, f32[512,256]{1,0:T(8,128)}, f32[512,512]{1,0:T(8,128)}) custom-call(f32[2,2,512,512]{3,2,1,0:T(8,128)} %maps.1, f32[2,2,1,512]{3,2,1,0:T(1,128)} %broadcast_in_dim.9.fluxes), custom_call_target="tpu_custom_call" | custom-call | flops 1000000000 | bytes 8404992 | tf_op jit(solution)/shard_map/pallas_call | solution.py:121
  29.3 4.1 %collective-permute-start.1 = (f32[264,256]{1,0:T(8,128)}, f32[264,256]{1,0:T(8,128)S(1)}, u32[]{:S(2)}, u32[]{:S(2)}) collective-permute-start(f32[264,256]{1,0:T(8,128)} %get-tuple-element.31.one.radial), channel_id=1, source_target_pairs={{0,2},{1,3},{2,0},{3,1},{4,6},{5,7},{6,4},{7,5},{8,10},{9,11},{10,... | collective-permute-start | bytes 811016 | tf_op jit(solution)/shard_map/ppermute | solution.py:20
  33.4 12.5 %collective-permute-done.1.two.radial_far = f32[264,256]{1,0:T(8,128)S(1)} collective-permute-done((f32[264,256]{1,0:T(8,128)}, f32[264,256]{1,0:T(8,128)S(1)}, u32[]{:S(2)}, u32[]{:S(2)}) %collective-permute-start.1) | collective-permute-done | bytes 270368 | tf_op jit(solution)/shard_map/ppermute | solution.py:20
  45.9 1.5 collective-permute-start
  47.4 6.2 %collective-permute-done = f32[256,256]{1,0:T(8,128)S(1)} collective-permute-done((f32[256,256]{1,0:T(8,128)}, f32[256,256]{1,0:T(8,128)S(1)}, u32[]{:S(2)}, u32[]{:S(2)}) %collective-permute-start) | collective-permute-done | bytes 262176 | tf_op jit(solution)/shard_map/ppermute | solution.py:20
  53.6 1.0 add.3.meet
  54.6 11.5 %shard_map.42 = (f32[256,256]{1,0:T(8,128)}, f32[1,256]{1,0:T(1,128)}) custom-call(f32[264,256]{1,0:T(8,128)} %get-tuple-element.31.one.radial, f32[264,256]{1,0:T(8,128)} %copy-done.8), custom_call_target="tpu_custom_call" | custom-call | flops 4000000000 | bytes 1081344 | tf_op jit(solution)/shard_map/pallas_call | solution.py:121
  66.1 16.5 %collective-permute-done.2.rest_far = f32[768,256]{1,0:T(8,128)S(1)} collective-permute-done((f32[768,256]{1,0:T(8,128)}, f32[768,256]{1,0:T(8,128)S(1)}, u32[]{:S(2)}, u32[]{:S(2)}) %collective-permute-start.2) | collective-permute-done | bytes 786464 | tf_op jit(solution)/shard_map/ppermute | solution.py:20
  82.6 0.9 copy-done.3
  83.4 4.1 %shard_map.43 = (f32[520,256]{1,0:T(8,128)}, f32[2,512,256]{2,1,0:T(8,128)}, f32[1,512]{1,0:T(1,128)}) custom-call(f32[256,256]{1,0:T(8,128)} %get-tuple-element.38.inverse, f32[1,256]{1,0:T(1,128)} %get-tuple-element.39.solved, f32[264,256]{1,0:T(8,128)} %get-tuple-element.31.one.radial, f32[264,256]{1,0:T(8,128)} %copy-done.8, ...), custom_call_target="tpu_custom_call" | custom-call | flops 1000000000 | bytes 4753408 | tf_op jit(solution)/shard_map/pallas_call | solution.py:121
  87.5 1.3 collective-permute-start.4
  88.8 11.3 %collective-permute-done.4.thin_far = f32[520,256]{1,0:T(8,128)S(1)} collective-permute-done((f32[520,256]{1,0:T(8,128)}, f32[520,256]{1,0:T(8,128)S(1)}, u32[]{:S(2)}, u32[]{:S(2)}) %collective-permute-start.4) | collective-permute-done | bytes 532512 | tf_op jit(solution)/shard_map/ppermute | solution.py:20
  100.1 1.0 collective-permute-start.7
  101.1 1.1 collective-permute-start.8
  102.1 0.7 copy-done.9
  102.8 26.7 %shard_map.44 = (f32[512,512]{1,0:T(8,128)}, f32[1,512]{1,0:T(1,128)}, f32[512,256]{1,0:T(8,128)}, f32[512,256]{1,0:T(8,128)}) custom-call(f32[256,256]{1,0:T(8,128)} %copy-done.2, f32[256,256]{1,0:T(8,128)} %copy-done.9, f32[520,256]{1,0:T(8,128)} %get-tuple-element.41.thin, f32[520,256]{1,0:T(8,128)} %copy-done.4), custom_call_target="tpu_custom_call" | custom-call | flops 8000000000 | bytes 3178496 | tf_op jit(solution)/shard_map/pallas_call | solution.py:121
  129.6 1.0 collective-permute-start.6
  130.6 6.6 %collective-permute-done.8.side_ax = f32[512,256]{1,0:T(8,128)S(1)} collective-permute-done((f32[512,256]{1,0:T(8,128)S(1)}, f32[512,256]{1,0:T(8,128)S(1)}, u32[]{:S(2)}, u32[]{:S(2)}) %collective-permute-start.8) | collective-permute-done | bytes 524320 | tf_op jit(solution)/shard_map/ppermute | solution.py:20
  137.2 0.8 copy-done.6
  138.0 0.4 copy-done
  138.4 7.0 %shard_map.45 = (f32[3,512,512]{2,1,0:T(8,128)}, f32[1,512]{1,0:T(1,128)}) custom-call(f32[512,512]{1,0:T(8,128)} %get-tuple-element.46.inverse, f32[1,512]{1,0:T(1,128)} %get-tuple-element.50.solved, f32[512,256]{1,0:T(8,128)} %get-tuple-element.51.bent, f32[512,256]{1,0:T(8,128)} %get-tuple-element.47.bent_far, f32[512,256]{1,0:T(8,128)} %get-tuple-element.45.side, ...), custom_call_target="tpu_custom_call" | custom-call | flops 4000000000 | bytes 11542528 | tf_op jit(solution)/shard_map/pallas_call | solution.py:121
  145.4 0.8 copy-done.1
  146.2 12.0 %shard_map.46 = (f32[512,2048]{1,0:T(8,128)}, f32[1,512]{1,0:T(1,128)}) custom-call(f32[512,512]{1,0:T(8,128)} %get-tuple-element.46.inverse, f32[512,256]{1,0:T(8,128)} %get-tuple-element.47.bent_far, f32[512,256]{1,0:T(8,128)} %copy-done.1, f32[2,512,256]{2,1,0:T(8,128)} %get-tuple-element.49.scaled, f32[2,512,256]{2,1,0:T(8,128)} %copy-done, ...), custom_call_target="tpu_custom_call" | custom-call | flops 1000000000 | bytes 16781312 | tf_op jit(solution)/shard_map/pallas_call | solution.py:121
  (22 shorter events, 0.0 us)
Async XLA Ops:
  29.3 16.5 %collective-permute-start.1 = (f32[264,256]{1,0:T(8,128)}, f32[264,256]{1,0:T(8,128)S(1)}, u32[]{:S(2)}, u32[]{:S(2)}) collective-permute-start(f32[264,256]{1,0:T(8,128)} %get-tuple-element.31.one.radial), channel_id=1, source_target_pairs={{0,2},{1,3},{2,0},{3,1},{4,6},{5,7},{6,4},{7,5},{8,10},{9,11},{10,... | collective-permute-start | bytes 811016 | tf_op jit(solution)/shard_map/ppermute | solution.py:20
  45.9 8.7 %copy-start.8 = (f32[264,256]{1,0:T(8,128)}, f32[264,256]{1,0:T(8,128)S(1)}, u32[]{:S(2)}) copy-start(f32[264,256]{1,0:T(8,128)S(1)} %collective-permute-done.1.two.radial_far) | copy-start | bytes 811012
  45.9 36.7 %collective-permute-start.2 = (f32[768,256]{1,0:T(8,128)}, f32[768,256]{1,0:T(8,128)S(1)}, u32[]{:S(2)}, u32[]{:S(2)}) collective-permute-start(f32[768,256]{1,0:T(8,128)} %get-tuple-element.33.rest), channel_id=1, source_target_pairs={{0,2},{1,3},{2,0},{3,1},{4,6},{5,7},{6,4},{7,5},{8,10},{9,11},{10,... | collective-permute-start | bytes 2359304 | tf_op jit(solution)/shard_map/ppermute | solution.py:20
  45.9 7.7 %collective-permute-start = (f32[256,256]{1,0:T(8,128)}, f32[256,256]{1,0:T(8,128)S(1)}, u32[]{:S(2)}, u32[]{:S(2)}) collective-permute-start(f32[256,256]{1,0:T(8,128)} %get-tuple-element.30), channel_id=1, source_target_pairs={{0,16},{4,20},{8,24},{12,28},{16,0},{20,4},{24,8},{28,12},{1,17},{... | collective-permute-start | bytes 786440 | tf_op jit(solution)/shard_map/ppermute | solution.py:20
  54.6 34.2 %copy-start.2 = (f32[256,256]{1,0:T(8,128)}, f32[256,256]{1,0:T(8,128)S(1)}, u32[]{:S(2)}) copy-start(f32[256,256]{1,0:T(8,128)S(1)} %add.3.meet) | copy-start | bytes 786436
  54.6 46.5 %copy-start.5 = (f32[512,256]{1,0:T(8,128)S(1)}, f32[512,256]{1,0:T(8,128)}, u32[]{:S(2)}) copy-start(f32[512,256]{1,0:T(8,128)} %get-tuple-element.45.side) | copy-start | bytes 1572868
  82.6 0.9 copy-start.3
  87.5 12.6 %collective-permute-start.4 = (f32[520,256]{1,0:T(8,128)}, f32[520,256]{1,0:T(8,128)S(1)}, u32[]{:S(2)}, u32[]{:S(2)}) collective-permute-start(f32[520,256]{1,0:T(8,128)} %get-tuple-element.41.thin), channel_id=1, source_target_pairs={{0,16},{4,20},{8,24},{12,28},{16,0},{20,4},{24,8},{28,12},{1,17},{... | collective-permute-start | bytes 1597448 | tf_op jit(solution)/shard_map/ppermute | solution.py:20
  88.8 13.4 %collective-permute-start.3 = (f32[256,256]{1,0:T(8,128)S(1)}, f32[256,256]{1,0:T(8,128)S(1)}, u32[]{:S(2)}, u32[]{:S(2)}) collective-permute-start(f32[256,256]{1,0:T(8,128)S(1)} %add.3.meet), channel_id=1, source_target_pairs={{0,2},{1,3},{2,0},{3,1},{4,6},{5,7},{6,4},{7,5},{8,10},{9,11},{10,... | collective-permute-start | bytes 786440 | tf_op jit(solution)/shard_map/ppermute | solution.py:20
  100.1 2.0 %copy-start.4 = (f32[520,256]{1,0:T(8,128)}, f32[520,256]{1,0:T(8,128)S(1)}, u32[]{:S(2)}) copy-start(f32[520,256]{1,0:T(8,128)S(1)} %collective-permute-done.4.thin_far) | copy-start | bytes 1597444
  100.1 37.1 %collective-permute-start.7 = (f32[2,512,256]{2,1,0:T(8,128)}, f32[2,512,256]{2,1,0:T(8,128)S(1)}, u32[]{:S(2)}, u32[]{:S(2)}) collective-permute-start(f32[2,512,256]{2,1,0:T(8,128)} %get-tuple-element.49.scaled), channel_id=1, source_target_pairs={{0,16},{4,20},{8,24},{12,28},{16,0},{20,4},{24,8},{28,12},{1,17},{... | collective-permute-start | bytes 3145736 | tf_op jit(solution)/shard_map/ppermute | solution.py:20
  101.1 36.2 %collective-permute-start.8 = (f32[512,256]{1,0:T(8,128)S(1)}, f32[512,256]{1,0:T(8,128)S(1)}, u32[]{:S(2)}, u32[]{:S(2)}) collective-permute-start(f32[512,256]{1,0:T(8,128)S(1)} %copy-done.5), channel_id=1, source_target_pairs={{0,16},{4,20},{8,24},{12,28},{16,0},{20,4},{24,8},{28,12},{1,17},{... | collective-permute-start | bytes 1572872 | tf_op jit(solution)/shard_map/ppermute | solution.py:20
  102.1 0.7 copy-start.9
  102.1 27.4 %collective-permute-start.5 = (f32[512,256]{1,0:T(8,128)S(1)}, f32[512,256]{1,0:T(8,128)S(1)}, u32[]{:S(2)}, u32[]{:S(2)}) collective-permute-start(f32[512,256]{1,0:T(8,128)S(1)} %copy-done.5), channel_id=1, source_target_pairs={{0,2},{1,3},{2,0},{3,1},{4,6},{5,7},{6,4},{7,5},{8,10},{9,11},{10,... | collective-permute-start | bytes 1572872 | tf_op jit(solution)/shard_map/ppermute | solution.py:20
  129.6 7.7 %copy-start.7 = (f32[512,256]{1,0:T(8,128)}, f32[512,256]{1,0:T(8,128)S(1)}, u32[]{:S(2)}) copy-start(f32[512,256]{1,0:T(8,128)S(1)} %collective-permute-done.5.side_rad) | copy-start | bytes 1572868
  129.6 15.9 %collective-permute-start.6 = (f32[512,256]{1,0:T(8,128)S(1)}, f32[512,256]{1,0:T(8,128)S(1)}, u32[]{:S(2)}, u32[]{:S(2)}) collective-permute-start(f32[512,256]{1,0:T(8,128)S(1)} %collective-permute-done.5.side_rad), channel_id=1, source_target_pairs={{0,16},{4,20},{8,24},{12,28},{16,0},{20,4},{24,8},{28,12},{1,17},{... | collective-permute-start | bytes 1572872 | tf_op jit(solution)/shard_map/ppermute | solution.py:20
  137.2 0.8 copy-start.6
  137.2 1.2 copy-start
  145.4 0.8 copy-start.1

commit v4 on v3

--- a/solution.py
+++ b/solution.py
@@ -322,11 +322,11 @@
     radial_far = swapped(radial, "rad")
     meet_ax = swapped(meet, "ax")
     side_ax = swapped(side, "ax")
-    radial_far, rest_late = after(radial_far, rest)
-    rest_far = swapped(rest_late, "rad")
+    rest_far = swapped(rest, "rad")
     inverse, solved = call(
         factor_kernel, [(n, n), (1, n)], [(n, m)], 4 * 10**9, radial, radial_far
     )
+    inverse, meet_ax, side_ax = lax.optimization_barrier((inverse, meet_ax, side_ax))
     meet_sum = meet + meet_ax
     rest_far, meet_late = after(rest_far, meet_sum)
     meet_far = swapped(meet_late, "rad")

time: 158 us -> 166 us (1.051); the launches traced: 158 us -> 164 us
  waiting for transfers between devices: 53.1 us -> 59.4 us
    ppermute x9, waiting for transfers between devices: 53.1 us -> 59.4 us  [swapped(): return lax.ppermute(value, axis, pairs)]
    unnamed x20 -> x22, local copies, waits for them, and re-layouts: 3.54 us -> 4.04 us
  transfers between devices with their start and end apart: 9 -> 9, of which waited for: 5 -> 4; matrix products, arithmetic and copies ran while one was open for 1% -> 0% of each run, Pallas kernels for 29% -> 28%
where the time goes in v4:
time: 166 us; the launch traced here: 164 us
  Pallas kernels  88.6 us (53%)
  waiting for transfers between devices  59.4 us (36%)
  starting transfers between devices  9.77 us (6%)
  local copies, waits for them, and re-layouts  5.34 us (3%)
    pallas_call x6, Pallas kernels, call(): pl.pallas_call(kernel, out_shape=[jax.ShapeDtypeStruct(s, F32) for s in s...  88.6 us
    ppermute x9, waiting for transfers between devices, swapped(): return lax.ppermute(value, axis, pairs)  59.4 us
    ppermute x9, starting transfers between devices, swapped(): return lax.ppermute(value, axis, pairs)  9.77 us
    unnamed x22, local copies, waits for them, and re-layouts  4.04 us
  transfers between devices with their start and end apart: 9, of which 4 were waited for; matrix products, arithmetic and copies ran while one was open for 0% of the time, Pallas kernels for 28%

profile of v4, /device:TPU:0, one launch (start us, length us, event | category | flops | bytes accessed | tf_op | source)
XLA Modules:
  0.0 163.9 jit_solution(7465788708496596886)
XLA Ops:
  0.6 1.3 broadcast_in_dim.9.fluxes
  1.9 27.4 %shard_map.41 = (f32[264,256]{1,0:T(8,128)}, f32[768,256]{1,0:T(8,128)}, f32[256,256]{1,0:T(8,128)}, f32[512,256]{1,0:T(8,128)}, f32[512,512]{1,0:T(8,128)}) custom-call(f32[2,2,512,512]{3,2,1,0:T(8,128)} %maps.1, f32[2,2,1,512]{3,2,1,0:T(1,128)} %broadcast_in_dim.9.fluxes), custom_call_target="tpu_custom_call" | custom-call | flops 1000000000 | bytes 8404992 | tf_op jit(solution)/shard_map/pallas_call | solution.py:121
  29.3 4.1 %collective-permute-start.3 = (f32[768,256]{1,0:T(8,128)}, f32[768,256]{1,0:T(8,128)S(1)}, u32[]{:S(2)}, u32[]{:S(2)}) collective-permute-start(f32[768,256]{1,0:T(8,128)} %get-tuple-element.36.rest), channel_id=1, source_target_pairs={{0,2},{1,3},{2,0},{3,1},{4,6},{5,7},{6,4},{7,5},{8,10},{9,11},{10,... | collective-permute-start | bytes 2359304 | tf_op jit(solution)/shard_map/ppermute | solution.py:20
  33.4 0.0 collective-permute-start
  33.4 1.8 %collective-permute-start.2 = (f32[512,256]{1,0:T(8,128)}, f32[512,256]{1,0:T(8,128)S(1)}, u32[]{:S(2)}, u32[]{:S(2)}) collective-permute-start(f32[512,256]{1,0:T(8,128)} %get-tuple-element.46.side), channel_id=1, source_target_pairs={{0,16},{4,20},{8,24},{12,28},{16,0},{20,4},{24,8},{28,12},{1,17},{... | collective-permute-start | bytes 1572872 | tf_op jit(solution)/shard_map/ppermute | solution.py:20
  35.2 0.2 collective-permute-start.1
  35.4 44.1 %collective-permute-done.two.radial_far = f32[264,256]{1,0:T(8,128)S(1)} collective-permute-done((f32[264,256]{1,0:T(8,128)}, f32[264,256]{1,0:T(8,128)S(1)}, u32[]{:S(2)}, u32[]{:S(2)}) %collective-permute-start) | collective-permute-done | bytes 270368 | tf_op jit(solution)/shard_map/ppermute | solution.py:20
  79.6 0.7 copy-done.9
  80.3 11.4 %shard_map.42 = (f32[256,256]{1,0:T(8,128)}, f32[1,256]{1,0:T(1,128)}) custom-call(f32[264,256]{1,0:T(8,128)} %get-tuple-element.32.one.radial, f32[264,256]{1,0:T(8,128)} %copy-done.9), custom_call_target="tpu_custom_call" | custom-call | flops 4000000000 | bytes 1081344 | tf_op jit(solution)/shard_map/pallas_call | solution.py:121
  91.7 0.9 copy-done.4
  92.6 4.1 %shard_map.43 = (f32[520,256]{1,0:T(8,128)}, f32[2,512,256]{2,1,0:T(8,128)}, f32[1,512]{1,0:T(1,128)}) custom-call(f32[256,256]{1,0:T(8,128)} %get-tuple-element.39.inverse, f32[1,256]{1,0:T(1,128)} %get-tuple-element.40.solved, f32[264,256]{1,0:T(8,128)} %get-tuple-element.32.one.radial, f32[264,256]{1,0:T(8,128)} %copy-done.9, ...), custom_call_target="tpu_custom_call" | custom-call | flops 1000000000 | bytes 4753408 | tf_op jit(solution)/shard_map/pallas_call | solution.py:121
  96.7 1.6 collective-permute-start.5
  98.2 11.9 %collective-permute-done.5.thin_far = f32[520,256]{1,0:T(8,128)S(1)} collective-permute-done((f32[520,256]{1,0:T(8,128)}, f32[520,256]{1,0:T(8,128)S(1)}, u32[]{:S(2)}, u32[]{:S(2)}) %collective-permute-start.5) | collective-permute-done | bytes 532512 | tf_op jit(solution)/shard_map/ppermute | solution.py:20
  110.2 1.3 collective-permute-start.8
  111.4 0.2 collective-permute-done.4.meet_far
  111.7 0.7 copy-done.10
  112.4 26.8 %shard_map.44 = (f32[512,512]{1,0:T(8,128)}, f32[1,512]{1,0:T(1,128)}, f32[512,256]{1,0:T(8,128)}, f32[512,256]{1,0:T(8,128)}) custom-call(f32[256,256]{1,0:T(8,128)} %copy-done.2, f32[256,256]{1,0:T(8,128)} %copy-done.10, f32[520,256]{1,0:T(8,128)} %get-tuple-element.42.thin, f32[520,256]{1,0:T(8,128)} %copy-done.5), custom_call_target="tpu_custom_call" | custom-call | flops 8000000000 | bytes 3178496 | tf_op jit(solution)/shard_map/pallas_call | solution.py:121
  139.1 0.0 copy-start.8
  139.2 0.8 collective-permute-start.7
  140.0 1.0 copy-done
  141.0 7.0 %shard_map.45 = (f32[3,512,512]{2,1,0:T(8,128)}, f32[1,512]{1,0:T(1,128)}) custom-call(f32[512,512]{1,0:T(8,128)} %get-tuple-element.47.inverse, f32[1,512]{1,0:T(1,128)} %get-tuple-element.51.solved, f32[512,256]{1,0:T(8,128)} %get-tuple-element.52.bent, f32[512,256]{1,0:T(8,128)} %get-tuple-element.48.bent_far, f32[512,256]{1,0:T(8,128)} %get-tuple-element.46.side, ...), custom_call_target="tpu_custom_call" | custom-call | flops 4000000000 | bytes 11542528 | tf_op jit(solution)/shard_map/pallas_call | solution.py:121
  148.0 3.1 %collective-permute-done.7.side_diag = f32[512,256]{1,0:T(8,128)S(1)} collective-permute-done((f32[512,256]{1,0:T(8,128)S(1)}, f32[512,256]{1,0:T(8,128)S(1)}, u32[]{:S(2)}, u32[]{:S(2)}) %collective-permute-start.7) | collective-permute-done | bytes 524320 | tf_op jit(solution)/shard_map/ppermute | solution.py:20
  151.1 0.8 copy-done.1
  151.9 12.0 %shard_map.46 = (f32[512,2048]{1,0:T(8,128)}, f32[1,512]{1,0:T(1,128)}) custom-call(f32[512,512]{1,0:T(8,128)} %get-tuple-element.47.inverse, f32[512,256]{1,0:T(8,128)} %get-tuple-element.48.bent_far, f32[512,256]{1,0:T(8,128)} %copy-done.1, f32[2,512,256]{2,1,0:T(8,128)} %get-tuple-element.50.scaled, f32[2,512,256]{2,1,0:T(8,128)} %copy-done, ...), custom_call_target="tpu_custom_call" | custom-call | flops 1000000000 | bytes 16781312 | tf_op jit(solution)/shard_map/pallas_call | solution.py:121
  (24 shorter events, 0.1 us)
Async XLA Ops:
  29.3 62.4 %collective-permute-start.3 = (f32[768,256]{1,0:T(8,128)}, f32[768,256]{1,0:T(8,128)S(1)}, u32[]{:S(2)}, u32[]{:S(2)}) collective-permute-start(f32[768,256]{1,0:T(8,128)} %get-tuple-element.36.rest), channel_id=1, source_target_pairs={{0,2},{1,3},{2,0},{3,1},{4,6},{5,7},{6,4},{7,5},{8,10},{9,11},{10,... | collective-permute-start | bytes 2359304 | tf_op jit(solution)/shard_map/ppermute | solution.py:20
  33.4 46.2 %collective-permute-start = (f32[264,256]{1,0:T(8,128)}, f32[264,256]{1,0:T(8,128)S(1)}, u32[]{:S(2)}, u32[]{:S(2)}) collective-permute-start(f32[264,256]{1,0:T(8,128)} %get-tuple-element.32.one.radial), channel_id=1, source_target_pairs={{0,2},{1,3},{2,0},{3,1},{4,6},{5,7},{6,4},{7,5},{8,10},{9,11},{10,... | collective-permute-start | bytes 811016 | tf_op jit(solution)/shard_map/ppermute | solution.py:20
  33.4 58.2 %collective-permute-start.2 = (f32[512,256]{1,0:T(8,128)}, f32[512,256]{1,0:T(8,128)S(1)}, u32[]{:S(2)}, u32[]{:S(2)}) collective-permute-start(f32[512,256]{1,0:T(8,128)} %get-tuple-element.46.side), channel_id=1, source_target_pairs={{0,16},{4,20},{8,24},{12,28},{16,0},{20,4},{24,8},{28,12},{1,17},{... | collective-permute-start | bytes 1572872 | tf_op jit(solution)/shard_map/ppermute | solution.py:20
  35.2 56.5 %copy-start.3 = (f32[256,256]{1,0:T(8,128)S(1)}, f32[256,256]{1,0:T(8,128)}, u32[]{:S(2)}) copy-start(f32[256,256]{1,0:T(8,128)} %get-tuple-element.31) | copy-start | bytes 786436
  35.2 56.4 %collective-permute-start.1 = (f32[256,256]{1,0:T(8,128)}, f32[256,256]{1,0:T(8,128)S(1)}, u32[]{:S(2)}, u32[]{:S(2)}) collective-permute-start(f32[256,256]{1,0:T(8,128)} %get-tuple-element.31), channel_id=1, source_target_pairs={{0,16},{4,20},{8,24},{12,28},{16,0},{20,4},{24,8},{28,12},{1,17},{... | collective-permute-start | bytes 786440 | tf_op jit(solution)/shard_map/ppermute | solution.py:20
  79.6 0.7 copy-start.9
  91.6 20.0 %copy-start.6 = (f32[512,256]{1,0:T(8,128)S(1)}, f32[512,256]{1,0:T(8,128)}, u32[]{:S(2)}) copy-start(f32[512,256]{1,0:T(8,128)} %get-tuple-element.46.side) | copy-start | bytes 1572868
  91.7 47.5 %copy-start.7 = (f32[512,256]{1,0:T(8,128)}, f32[512,256]{1,0:T(8,128)S(1)}, u32[]{:S(2)}) copy-start(f32[512,256]{1,0:T(8,128)S(1)} %collective-permute-done.2.side_ax) | copy-start | bytes 1572868
  91.7 20.0 %copy-start.2 = (f32[256,256]{1,0:T(8,128)}, f32[256,256]{1,0:T(8,128)S(1)}, u32[]{:S(2)}) copy-start(f32[256,256]{1,0:T(8,128)S(1)} %add.3.meet) | copy-start | bytes 786436
  91.7 0.9 copy-start.4
  96.7 13.5 %collective-permute-start.5 = (f32[520,256]{1,0:T(8,128)}, f32[520,256]{1,0:T(8,128)S(1)}, u32[]{:S(2)}, u32[]{:S(2)}) collective-permute-start(f32[520,256]{1,0:T(8,128)} %get-tuple-element.42.thin), channel_id=1, source_target_pairs={{0,16},{4,20},{8,24},{12,28},{16,0},{20,4},{24,8},{28,12},{1,17},{... | collective-permute-start | bytes 1597448 | tf_op jit(solution)/shard_map/ppermute | solution.py:20
  98.2 13.4 %collective-permute-start.4 = (f32[256,256]{1,0:T(8,128)S(1)}, f32[256,256]{1,0:T(8,128)S(1)}, u32[]{:S(2)}, u32[]{:S(2)}) collective-permute-start(f32[256,256]{1,0:T(8,128)S(1)} %add.3.meet), channel_id=1, source_target_pairs={{0,2},{1,3},{2,0},{3,1},{4,6},{5,7},{6,4},{7,5},{8,10},{9,11},{10,... | collective-permute-start | bytes 786440 | tf_op jit(solution)/shard_map/ppermute | solution.py:20
  110.2 1.5 copy-start.5
  110.2 29.8 %collective-permute-start.8 = (f32[2,512,256]{2,1,0:T(8,128)}, f32[2,512,256]{2,1,0:T(8,128)S(1)}, u32[]{:S(2)}, u32[]{:S(2)}) collective-permute-start(f32[2,512,256]{2,1,0:T(8,128)} %get-tuple-element.50.scaled), channel_id=1, source_target_pairs={{0,16},{4,20},{8,24},{12,28},{16,0},{20,4},{24,8},{28,12},{1,17},{... | collective-permute-start | bytes 3145736 | tf_op jit(solution)/shard_map/ppermute | solution.py:20
  111.7 0.7 copy-start.10
  111.7 27.5 %collective-permute-start.6 = (f32[512,256]{1,0:T(8,128)S(1)}, f32[512,256]{1,0:T(8,128)S(1)}, u32[]{:S(2)}, u32[]{:S(2)}) collective-permute-start(f32[512,256]{1,0:T(8,128)S(1)} %copy-done.6), channel_id=1, source_target_pairs={{0,2},{1,3},{2,0},{3,1},{4,6},{5,7},{6,4},{7,5},{8,10},{9,11},{10,... | collective-permute-start | bytes 1572872 | tf_op jit(solution)/shard_map/ppermute | solution.py:20
  139.1 0.8 copy-start.8
  139.2 12.0 %collective-permute-start.7 = (f32[512,256]{1,0:T(8,128)S(1)}, f32[512,256]{1,0:T(8,128)S(1)}, u32[]{:S(2)}, u32[]{:S(2)}) collective-permute-start(f32[512,256]{1,0:T(8,128)S(1)} %collective-permute-done.6.side_rad), channel_id=1, source_target_pairs={{0,16},{4,20},{8,24},{12,28},{16,0},{20,4},{24,8},{28,12},{1,17},{... | collective-permute-start | bytes 1572872 | tf_op jit(solution)/shard_map/ppermute | solution.py:20
  140.0 1.0 copy-start
  151.1 0.8 copy-start.1
